TPU v7x, 32 devices: a whole 2x2x4 slice. The times are simulated.
32 devices in a mesh: dp: 4 (over y, core), tensor: 8 (over z, x).
Axes of the slice: x: 2, y: 2, z: 4, core: 2. Of those that a mesh axis runs over, the one named last changes fastest.
Arguments:
- loader_rows: bfloat16 [4, 8, 128, 4096], P('dp', 'tensor'), may hold values from -23 to 23
- row_counts: int32 [4, 8], P('dp', 'tensor'), may hold values from 0 to 128
- row_targets: int32 [4, 8, 128], P('dp', 'tensor'), may hold values from 0 to 255, as said below
- gate_weight: bfloat16 [4096, 16384], P('dp', 'tensor'), may hold values from -0.09375 to 0.09375
- up_weight: bfloat16 [4096, 16384], P('dp', 'tensor'), may hold values from -0.09375 to 0.09375
- down_weight: bfloat16 [16384, 4096], P('tensor'), may hold values from -0.046875 to 0.046875
Outputs:
- layer_out: bfloat16 [2048, 4096], P(('dp', 'tensor'))
Inputs may be any that keep to these rules, and one draw needn't show every extreme that they name: `row_targets`: among the first row_counts[d, t] slots of replica d and tensor index t, a value v names row v % 64 of the rows of tensor index t on replica v // 64; over all replicas each such row is named exactly once, and no device names more than 32 rows of one replica. Slots past the count hold arbitrary values of the same range.
All inputs are finite; a program needn't handle non-finite values.
Results may differ from a plain program's by a relative error of at most 0.0095.
Values may be sent and summed in bfloat16 or wider, within the bound.
A program may use at most 128 MiB of HBM per device.

v0:
```python
import jax
import jax.numpy as jnp
from jax import lax
from jax.sharding import PartitionSpec as P

ROWS_GRP = 512


def swiglu(inputs, gate_full, up_full):
    gate_act = jnp.dot(inputs, gate_full, preferred_element_type=jnp.float32)
    up_act = jnp.dot(inputs, up_full, preferred_element_type=jnp.float32)
    return (jax.nn.silu(gate_act) * up_act).astype(jnp.bfloat16)


def normalize(row_block):
    wide_rows = row_block.astype(jnp.float32)
    return (
        wide_rows * lax.rsqrt(jnp.mean(wide_rows * wide_rows, axis=1, keepdims=True) + 1e-05)
    ).astype(jnp.bfloat16)


def rounded_term(hidden_part, weights):
    partial_sum = jnp.dot(hidden_part, weights, preferred_element_type=jnp.float32)
    return lax.optimization_barrier(partial_sum.astype(jnp.bfloat16)).astype(jnp.float32)


def per_device(loader_rows, row_counts, row_targets, gate_weight, up_weight, down_weight):
    dp_count = lax.axis_size("dp")
    tp_count = lax.axis_size("tensor")
    slot_rows = loader_rows[0, 0]
    slot_targets = row_targets[0, 0]
    live_count = row_counts[0, 0]
    slot_count = slot_rows.shape[0]
    feature_count = slot_rows.shape[1]
    per_peer = slot_count // dp_count
    shard_rows = ROWS_GRP // tp_count
    slot_index = jnp.arange(slot_count, dtype=jnp.int32)
    is_live = slot_index < live_count
    peer_index = slot_targets // shard_rows
    row_place = slot_targets % shard_rows
    peer_hot = (
        (peer_index[:, None] == jnp.arange(dp_count, dtype=jnp.int32)[None, :]) & is_live[:, None]
    ).astype(jnp.int32)
    earlier = jnp.cumsum(peer_hot, axis=0) - peer_hot
    slot_rank = jnp.sum(earlier * peer_hot, axis=1)
    send_slot = peer_index * per_peer + slot_rank
    pick_matrix = (send_slot[None, :] == slot_index[:, None]) & is_live[None, :]
    outgoing = jnp.dot(
        pick_matrix.astype(jnp.bfloat16), slot_rows, preferred_element_type=jnp.float32
    ).astype(jnp.bfloat16)
    out_place = jnp.sum(jnp.where(pick_matrix, row_place[None, :] + 1, 0), axis=1) - 1
    arrived, arrived_place = (
        lax.all_to_all(
            outgoing.reshape(dp_count, per_peer, feature_count),
            "dp",
            split_axis=0,
            concat_axis=0,
            tiled=True,
        ),
        lax.all_to_all(
            out_place.reshape(dp_count, per_peer), "dp", split_axis=0, concat_axis=0, tiled=True
        ),
    )
    land_matrix = (
        arrived_place.reshape(slot_count)[None, :]
        == jnp.arange(shard_rows, dtype=jnp.int32)[:, None]
    ).astype(jnp.bfloat16)
    local_batch = jnp.dot(
        land_matrix, arrived.reshape(slot_count, feature_count), preferred_element_type=jnp.float32
    ).astype(jnp.bfloat16)
    gate_full, up_full = (
        lax.all_gather(gate_weight, "dp", axis=0, tiled=True),
        lax.all_gather(up_weight, "dp", axis=0, tiled=True),
    )
    travelling = normalize(local_batch)
    hidden = swiglu(lax.all_gather(travelling, "tensor", axis=0, tiled=True), gate_full, up_full)
    summed = lax.psum_scatter(
        rounded_term(hidden, down_weight).astype(jnp.bfloat16),
        "tensor",
        scatter_dimension=0,
        tiled=True,
    ).astype(jnp.float32)
    return (local_batch.astype(jnp.float32) + summed).astype(jnp.bfloat16)


def solution(mesh):
    placed = (
        P("dp", "tensor", None, None),
        P("dp", "tensor"),
        P("dp", "tensor", None),
        P("dp", "tensor"),
        P("dp", "tensor"),
        P("tensor", None),
    )
    return jax.shard_map(
        per_device, mesh=mesh, in_specs=placed, out_specs=P(("dp", "tensor"), None), check_vma=False
    )
```

profile of v0, /device:TPU:0, one launch (start us, length us, event | category | flops | bytes accessed | tf_op | source)
XLA Modules:
  0.0 451.9 jit_solution(15265818163919751610)
XLA Ops:
  6.5 0.0 copy-start
  6.5 0.8 fusion.9
  8.0 0.1 fusion.3
  8.1 0.2 reduce_window_sum.11
  8.2 0.2 select_reduce_fusion.1
  8.4 0.1 select_reduce_fusion
  8.6 0.7 sub.18
  9.2 4.2 all-to-all-start
  13.5 0.0 copy-done
  13.5 1.4 convolution_convert_fusion.1
  14.9 2.3 all-to-all-done
  17.1 3.5 all-to-all-start.1
  20.7 0.0 all-gather.4.cloned.1.call-start
  20.7 0.5 broadcast.147
  21.2 0.7 reduce.3
  21.9 0.1 eq.49
  22.0 13.1 %all-to-all-done.1 = bf16[4,32,4096]{2,1,0:T(8,128)(2,1)S(1)} async-done(((bf16[4,32,4096]{2,1,0:T(8,128)(2,1)}), bf16[4,32,4096]{2,1,0:T(8,128)(2,1)S(1)}, u32[]{:S(2)}, u32[]{:S(2)}) %all-to-all-start.1) | async-done | bytes 1048608 | tf_op jit(solution)/shard_map/all_to_all | solution.py:53
  35.1 0.4 multiply_reduce_fusion
  35.5 0.9 multiply_convert_fusion.1
  36.4 0.0 all-gather.4.cloned.1.call-update
  36.4 0.0 all-gather.6.cloned.1.call-start
  36.5 0.7 all-gather.6.cloned.1.call-update
  37.2 0.0 all-gather.8.cloned.1.call-start
  37.2 0.7 all-gather.8.cloned.1.call-update
  37.9 0.0 reduce-scatter.2.cloned.1.call-start
  38.0 72.7 %all-gather.4.cloned.1.call-done = bf16[512,4096]{1,0:T(8,128)(2,1)} async-done(((bf16[64,4096]{1,0:T(8,128)(2,1)}), bf16[512,4096]{1,0:T(8,128)(2,1)}) %all-gather.4.cloned.1.call-update) | async-done | bytes 4194320 | tf_op jit(solution)/shard_map/all_gather | solution.py:76
  110.7 105.8 %all-gather.6.cloned.1.call-done = bf16[4096,2048]{1,0:T(8,128)(2,1)} async-done(((bf16[1024,2048]{1,0:T(8,128)(2,1)}), bf16[4096,2048]{1,0:T(8,128)(2,1)}) %all-gather.6.cloned.1.call-update) | async-done | bytes 16777232 | tf_op jit(solution)/shard_map/all_gather | solution.py:72
  216.5 15.0 %fusion.11 = f32[512,2048]{1,0:T(8,128)} fusion(bf16[512,4096]{1,0:T(8,128)(2,1)} %all-gather.4.cloned.1.call-done, bf16[4096,2048]{1,0:T(8,128)(2,1)} %all-gather.6.cloned.1.call-done), kind=kOutput, calls=%fused_computation.32 | convolution fusion | flops 8589934592 | bytes 25165824 | tf_op jit(solution)/shard_map/dot_general | solution.py:10
  231.5 92.5 %all-gather.8.cloned.1.call-done = bf16[4096,2048]{1,0:T(8,128)(2,1)} async-done(((bf16[1024,2048]{1,0:T(8,128)(2,1)}), bf16[4096,2048]{1,0:T(8,128)(2,1)}) %all-gather.8.cloned.1.call-update) | async-done | bytes 16777232 | tf_op jit(solution)/shard_map/all_gather | solution.py:73
  324.0 0.0 copy-start.1
  324.0 31.3 %convolution_convert_fusion = bf16[512,4096]{1,0:T(8,128)(2,1)} fusion(bf16[2048,4096]{1,0:T(8,128)(2,1)} %param.11, f32[512,2048]{1,0:T(8,128)} %fusion.11, bf16[512,4096]{1,0:T(8,128)(2,1)} %all-gather.4.cloned.1.call-done, bf16[4096,2048]{1,0:T(8,128)(2,1)} %all-gather.8.cloned.1.call-done), kind=kOutput, calls=%fused_computation | convolution fusion | flops 17188257792 | bytes 46137344 | tf_op jit(solution)/shard_map/dot_general | solution.py:23
  355.3 0.0 reduce-scatter.2.cloned.1.call-update
  355.4 88.0 %reduce-scatter.2.cloned.1.call-done = bf16[64,4096]{1,0:T(8,128)(2,1)} async-done(((bf16[512,4096]{1,0:T(8,128)(2,1)}), bf16[64,4096]{1,0:T(8,128)(2,1)}) %reduce-scatter.2.cloned.1.call-update) | async-done | bytes 524304 | tf_op jit(solution)/shard_map/reduce_scatter | solution.py:77
  443.4 1.9 add_convert_fusion
  445.3 0.0 copy-done.1
  (4 shorter events, 0.0 us)
Async XLA Ops:
  6.5 6.9 %copy-start = (bf16[1,1,128,4096]{3,2,1,0:T(8,128)(2,1)S(1)}, bf16[1,1,128,4096]{3,2,1,0:T(8,128)(2,1)}, u32[]{:S(2)}) copy-start(bf16[1,1,128,4096]{3,2,1,0:T(8,128)(2,1)} %param.6) | copy-start | bytes 3145732
  9.2 7.9 %all-to-all-start = ((s32[4,1,32]{2,1,0:T(1,128)}), s32[4,1,32]{2,1,0:T(1,128)S(1)}, u32[]{:S(2)}, u32[]{:S(2)}) async-start(s32[4,1,32]{2,1,0:T(1,128)} %bitcast.2), calls=%async_computation | async-start | bytes 4096 | tf_op jit(solution)/shard_map/all_to_all | solution.py:60
  17.1 18.0 %all-to-all-start.1 = ((bf16[4,32,4096]{2,1,0:T(8,128)(2,1)}), bf16[4,32,4096]{2,1,0:T(8,128)(2,1)S(1)}, u32[]{:S(2)}, u32[]{:S(2)}) async-start(bf16[4,32,4096]{2,1,0:T(8,128)(2,1)} %bitcast.4), calls=%async_computation.1 | async-start | bytes 2097152 | tf_op jit(solution)/shard_map/all_to_all | solution.py:53
  20.7 90.0 %all-gather.4.cloned.1.call-start = ((), (), s32[]{:S(2)}) async-start(), calls=%async_computation.3 | async-start | bytes 4718592 | tf_op jit(solution)/shard_map/all_gather | solution.py:76
  36.4 180.0 %all-gather.6.cloned.1.call-start = ((), (), s32[]{:S(2)}) async-start(), calls=%async_computation.4 | async-start | bytes 20971520 | tf_op jit(solution)/shard_map/all_gather | solution.py:72
  37.2 286.8 %all-gather.8.cloned.1.call-start = ((), (), s32[]{:S(2)}) async-start(), calls=%async_computation.5 | async-start | bytes 20971520 | tf_op jit(solution)/shard_map/all_gather | solution.py:73
  37.9 405.5 %reduce-scatter.2.cloned.1.call-start = ((), (), s32[]{:S(2)}) async-start(), calls=%async_computation.6 | async-start | bytes 4718592 | tf_op jit(solution)/shard_map/reduce_scatter | solution.py:77
  324.0 121.3 %copy-start.1 = (bf16[1,1,128,4096]{3,2,1,0:T(8,128)(2,1)S(1)}, bf16[1,1,128,4096]{3,2,1,0:T(8,128)(2,1)}, u32[]{:S(2)}) copy-start(bf16[1,1,128,4096]{3,2,1,0:T(8,128)(2,1)} %param.6) | copy-start | bytes 3145732
Sparse Core Ops, SparseCore 0:
  36.6 74.0 all-gather.3
  112.2 104.1 all-gather.5
  218.0 105.9 all-gather.7
  355.5 87.8 reduce-scatter.1
where the time goes:
time: 452 us
  waiting for transfers between devices  376 us (83%)
  matrix products  48.2 us (11%)
  between operations  13.8 us (3%)
  starting transfers between devices  7.91 us (2%)
  other arithmetic  4.86 us (1%)
    all_gather x1, waiting for transfers between devices, per_device(): lax.all_gather(gate_weight, 'dp', axis=0, tiled=True)  106 us
    all_gather x1, waiting for transfers between devices, per_device(): lax.all_gather(up_weight, 'dp', axis=0, tiled=True)  92.5 us
    reduce_scatter x1, waiting for transfers between devices, per_device(): lax.psum_scatter(rounded_term(hidden, down_weight).astype(jnp.bfloat16),...  88 us
    all_gather x1, waiting for transfers between devices, per_device(): lax.all_gather(travelling, 'tensor', axis=0, tiled=True)  72.7 us
    dot_general x1, matrix products, rounded_term(): jnp.dot(hidden_part, weights, preferred_element_type=jnp.float32)  31.3 us
    dot_general x1, matrix products, swiglu(): gate_act = jnp.dot(inputs, gate_full, preferred_element_type=jnp.float32)  15 us
    all_to_all x1, waiting for transfers between devices, per_device(): lax.all_to_all(outgoing.reshape(dp_count, per_peer, feature_count), 'dp',...  13.1 us
  transfers between devices with their start and end apart: 6, of which 6 were waited for; matrix products, arithmetic and copies ran while one was open for 4% of the time, Pallas kernels for 0%

commit v1 on v0

--- a/solution.py
+++ b/solution.py
@@ -24,7 +24,7 @@
     return lax.optimization_barrier(partial_sum.astype(jnp.bfloat16)).astype(jnp.float32)
 
 
-def per_device(loader_rows, row_counts, row_targets, gate_weight, up_weight, down_weight):
+def rebalance(loader_rows, row_counts, row_targets):
     dp_count = lax.axis_size("dp")
     tp_count = lax.axis_size("tensor")
     slot_rows = loader_rows[0, 0]
@@ -68,6 +68,11 @@
     local_batch = jnp.dot(
         land_matrix, arrived.reshape(slot_count, feature_count), preferred_element_type=jnp.float32
     ).astype(jnp.bfloat16)
+    return local_batch
+
+
+def gathered_plan(loader_rows, row_counts, row_targets, gate_weight, up_weight, down_weight):
+    local_batch = rebalance(loader_rows, row_counts, row_targets)
     gate_full, up_full = (
         lax.all_gather(gate_weight, "dp", axis=0, tiled=True),
         lax.all_gather(up_weight, "dp", axis=0, tiled=True),
@@ -83,6 +88,62 @@
     return (local_batch.astype(jnp.float32) + summed).astype(jnp.bfloat16)
 
 
+def swap(value, axis, mask):
+    size = lax.axis_size(axis)
+    return lax.ppermute(value, axis, [(i, i ^ mask) for i in range(size)])
+
+
+def column_block(rows, index, width):
+    return lax.dynamic_slice_in_dim(rows, index * width, width, axis=1)
+
+
+def chip_plan(loader_rows, row_counts, row_targets, gate_weight, up_weight, down_weight):
+    me = lax.axis_index("dp")
+    width = gate_weight.shape[0]
+    z_count = lax.axis_size("tensor") // 2
+    gate_half = jnp.concatenate([gate_weight, swap(gate_weight, "dp", 1)], axis=0)
+    up_half = jnp.concatenate([up_weight, swap(up_weight, "dp", 1)], axis=0)
+    local_batch = rebalance(loader_rows, row_counts, row_targets)
+    shard_rows = local_batch.shape[0]
+    travelling = normalize(local_batch)
+    mine = jnp.concatenate(
+        [column_block(travelling, me, width), column_block(travelling, me ^ 1, width)], axis=1
+    )
+    theirs = jnp.concatenate(
+        [column_block(travelling, me ^ 2, width), column_block(travelling, me ^ 3, width)], axis=1
+    )
+    block = jnp.concatenate([swap(theirs, "dp", 2), mine], axis=0)
+    blocks = [block] + [swap(block, "tensor", 2 * step) for step in range(1, z_count)]
+    total = local_batch.astype(jnp.float32)
+    for step in range(z_count):
+        near = blocks[step]
+        far = swap(near, "tensor", 1)
+        rows = jnp.concatenate(
+            [near[:shard_rows], far[:shard_rows], near[shard_rows:], far[shard_rows:]], axis=0
+        )
+        half = 2 * shard_rows
+        gate_act = jnp.dot(rows, gate_half, preferred_element_type=jnp.float32)
+        gate_other = swap(gate_act[:half].astype(jnp.bfloat16), "dp", 2)
+        up_act = jnp.dot(rows, up_half, preferred_element_type=jnp.float32)
+        up_other = swap(up_act[:half].astype(jnp.bfloat16), "dp", 2)
+        gate_sum = gate_act[half:] + gate_other.astype(jnp.float32)
+        up_sum = up_act[half:] + up_other.astype(jnp.float32)
+        hidden = (jax.nn.silu(gate_sum) * up_sum).astype(jnp.bfloat16)
+        term = jnp.dot(hidden, down_weight, preferred_element_type=jnp.float32).astype(jnp.bfloat16)
+        from_x = swap(term[shard_rows:], "tensor", 1)
+        pair_sum = term[:shard_rows].astype(jnp.float32) + from_x.astype(jnp.float32)
+        if step:
+            pair_sum = swap(pair_sum.astype(jnp.bfloat16), "tensor", 2 * step).astype(jnp.float32)
+        total = total + pair_sum
+    return total.astype(jnp.bfloat16)
+
+
+def per_device(*args):
+    if lax.axis_size("dp") == 4 and lax.axis_size("tensor") == 8:
+        return chip_plan(*args)
+    return gathered_plan(*args)
+
+
 def solution(mesh):
     placed = (
         P("dp", "tensor", None, None),

time: 452 us -> 275 us (0.61)
  waiting for transfers between devices: 376 us -> 141 us
  starting transfers between devices: 7.91 us -> 53.2 us
  between operations: 13.8 us -> 1.13 us
  matrix products: 48.2 us -> 60.5 us
  local copies, waits for them, and re-layouts: 1.27 us -> 11.8 us
    all_gather x3 -> x0, waiting for transfers between devices: 271 us -> none  [the longest x1 106 us: per_device(): lax.all_gather(gate_weight, 'dp', axis=0, tiled=True)]
    ppermute x0 -> x25, waiting for transfers between devices: none -> 125 us  [swap(): return lax.ppermute(value, axis, [(i, i ^ mask) for i in range(size)])]
    reduce_scatter x1 -> x0, waiting for transfers between devices: 88 us -> none  [per_device(): lax.psum_scatter(rounded_term(hidden, down_weight).astype(jnp.bfloat16),...]
    ppermute x0 -> x25, starting transfers between devices: none -> 45.5 us  [swap(): return lax.ppermute(value, axis, [(i, i ^ mask) for i in range(size)])]
    dot_general x4 -> x14, matrix products: 48.2 us -> 60.5 us  [the longest x4 34.7 us: chip_plan(): jnp.dot(hidden, down_weight, preferred_element_type=jnp.float32)]
    unnamed x4 -> x24, local copies, waits for them, and re-layouts: 0.01 us -> 5.42 us
  transfers between devices with their start and end apart: 6 -> 27, of which waited for: 6 -> 17; matrix products, arithmetic and copies ran while one was open for 4% -> 22% of each run, Pallas kernels for 0% -> 0%
where the time goes in v1:
time: 275 us; the launch traced here: 271 us
  waiting for transfers between devices  141 us (51%)
  matrix products  60.5 us (22%)
  starting transfers between devices  53.2 us (19%)
  local copies, waits for them, and re-layouts  11.8 us (4%)
  other arithmetic  3.77 us (1%)
    ppermute x25, waiting for transfers between devices, swap(): return lax.ppermute(value, axis, [(i, i ^ mask) for i in range(size)])  125 us
    ppermute x25, starting transfers between devices, swap(): return lax.ppermute(value, axis, [(i, i ^ mask) for i in range(size)])  45.5 us
    dot_general x4, matrix products, chip_plan(): jnp.dot(hidden, down_weight, preferred_element_type=jnp.float32)  34.7 us
    dot_general x4, matrix products, chip_plan(): gate_act = jnp.dot(rows, gate_half, preferred_element_type=jnp.float32)  14.3 us
    all_to_all x1, waiting for transfers between devices, rebalance(): lax.all_to_all(outgoing.reshape(dp_count, per_peer, feature_count), 'dp',...  13.1 us
    dot_general x4, matrix products, chip_plan(): up_act = jnp.dot(rows, up_half, preferred_element_type=jnp.float32)  9.78 us
  transfers between devices with their start and end apart: 27, of which 17 were waited for; matrix products, arithmetic and copies ran while one was open for 22% of the time, Pallas kernels for 0%

profile of v1, /device:TPU:0, one launch (start us, length us, event | category | flops | bytes accessed | tf_op | source)
XLA Modules:
  0.0 271.3 jit_solution(13216685704147611318)
XLA Ops:
  0.0 0.8 fusion.31
  2.0 0.7 sub.18
  2.7 4.2 %all-to-all-start = ((s32[4,1,32]{2,1,0:T(1,128)}), s32[4,1,32]{2,1,0:T(1,128)S(1)}, u32[]{:S(2)}, u32[]{:S(2)}) async-start(s32[4,1,32]{2,1,0:T(1,128)} %bitcast.2), calls=%async_computation | async-start | bytes 4096 | tf_op jit(solution)/shard_map/all_to_all | solution.py:60
  6.9 1.4 convolution_convert_fusion.4
  8.3 2.3 all-to-all-done
  10.6 3.5 %all-to-all-start.1 = ((bf16[4,32,4096]{2,1,0:T(8,128)(2,1)}), bf16[4,32,4096]{2,1,0:T(8,128)(2,1)S(1)}, u32[]{:S(2)}, u32[]{:S(2)}) async-start(bf16[4,32,4096]{2,1,0:T(8,128)(2,1)} %bitcast.4), calls=%async_computation.1 | async-start | bytes 2097152 | tf_op jit(solution)/shard_map/all_to_all | solution.py:53
  14.1 0.5 broadcast.150
  14.7 0.7 reduce.3
  15.4 13.1 %all-to-all-done.1 = bf16[4,32,4096]{2,1,0:T(8,128)(2,1)S(1)} async-done(((bf16[4,32,4096]{2,1,0:T(8,128)(2,1)}), bf16[4,32,4096]{2,1,0:T(8,128)(2,1)S(1)}, u32[]{:S(2)}, u32[]{:S(2)}) %all-to-all-start.1) | async-done | bytes 1048608 | tf_op jit(solution)/shard_map/all_to_all | solution.py:53
  29.6 1.1 copy-done.2
  31.3 5.8 %collective-permute-done = bf16[64,2048]{1,0:T(8,128)(2,1)S(1)} collective-permute-done((bf16[64,2048]{1,0:T(8,128)(2,1)S(1)}, bf16[64,2048]{1,0:T(8,128)(2,1)S(1)}, u32[]{:S(2)}, u32[]{:S(2)}) %collective-permute-start) | collective-permute-done | bytes 262176 | tf_op jit(solution)/shard_map/ppermute | solution.py:93
  37.1 2.0 collective-permute-start.7
  39.2 2.3 constant_dynamic-update-slice_fusion.1
  41.5 2.6 collective-permute-start.13
  44.1 0.6 constant_dynamic-update-slice_fusion.3
  44.7 1.6 collective-permute-start.1
  46.2 12.7 %collective-permute-done.7 = bf16[128,2048]{1,0:T(8,128)(2,1)S(1)} collective-permute-done((bf16[128,2048]{1,0:T(8,128)(2,1)S(1)}, bf16[128,2048]{1,0:T(8,128)(2,1)S(1)}, u32[]{:S(2)}, u32[]{:S(2)}) %collective-permute-start.7) | collective-permute-done | bytes 524320 | tf_op jit(solution)/shard_map/ppermute | solution.py:93
  58.9 2.5 collective-permute-start.19
  61.4 18.1 %collective-permute-done.13 = bf16[128,2048]{1,0:T(8,128)(2,1)S(1)} collective-permute-done((bf16[128,2048]{1,0:T(8,128)(2,1)S(1)}, bf16[128,2048]{1,0:T(8,128)(2,1)S(1)}, u32[]{:S(2)}, u32[]{:S(2)}) %collective-permute-start.13) | collective-permute-done | bytes 524320 | tf_op jit(solution)/shard_map/ppermute | solution.py:93
  79.5 1.5 collective-permute-start.8
  81.1 0.6 collective-permute-start.14
  81.7 1.5 collective-permute-start.20
  83.3 8.9 %collective-permute-done.8 = bf16[128,2048]{1,0:T(8,128)(2,1)S(1)} collective-permute-done((bf16[128,2048]{1,0:T(8,128)(2,1)S(1)}, bf16[128,2048]{1,0:T(8,128)(2,1)S(1)}, u32[]{:S(2)}, u32[]{:S(2)}) %collective-permute-start.8) | collective-permute-done | bytes 524320 | tf_op jit(solution)/shard_map/ppermute | solution.py:93
  92.2 5.6 %collective-permute-done.14 = bf16[128,2048]{1,0:T(8,128)(2,1)S(1)} collective-permute-done((bf16[128,2048]{1,0:T(8,128)(2,1)S(1)}, bf16[128,2048]{1,0:T(8,128)(2,1)S(1)}, u32[]{:S(2)}, u32[]{:S(2)}) %collective-permute-start.14) | collective-permute-done | bytes 524320 | tf_op jit(solution)/shard_map/ppermute | solution.py:93
  97.8 5.6 %collective-permute-done.20 = bf16[128,2048]{1,0:T(8,128)(2,1)S(1)} collective-permute-done((bf16[128,2048]{1,0:T(8,128)(2,1)S(1)}, bf16[128,2048]{1,0:T(8,128)(2,1)S(1)}, u32[]{:S(2)}, u32[]{:S(2)}) %collective-permute-start.20) | collective-permute-done | bytes 524320 | tf_op jit(solution)/shard_map/ppermute | solution.py:93
  103.5 2.3 constant_dynamic-update-slice_fusion
  105.8 7.1 %fusion.23 = f32[256,2048]{1,0:T(8,128)} fusion(bf16[2048,2048]{1,0:T(8,128)(2,1)} %constant_dynamic-update-slice_fusion, bf16[64,2048]{1,0:T(8,128)(2,1)S(1)} %get-tuple-element.10, bf16[64,2048]{1,0:T(8,128)(2,1)S(1)} %get-tuple-element.8, bf16[64,2048]{1,0:T(8,128)(2,1)S(1)} %get-tuple-element.9, bf16[64,2048]{1,0:T(8,128)(2,1)S(1)} %get-tuple-element.7), kind=kOutput, calls=%fused_computation.53 | convolution fusion | flops 2151677952 | bytes 11534336 | tf_op jit(solution)/shard_map/dot_general | solution.py:125
  112.9 0.6 constant_dynamic-update-slice_fusion.2
  113.5 2.4 fusion.22
  115.9 0.6 slice-done.1
  116.5 2.4 fusion.21
  118.9 2.4 fusion.20
  121.3 2.4 fusion.43
  123.8 9.0 %collective-permute-start.3 = (bf16[128,2048]{1,0:T(8,128)(2,1)S(1)}, bf16[128,2048]{1,0:T(8,128)(2,1)S(1)}, u32[]{:S(2)}, u32[]{:S(2)}) collective-permute-start(bf16[128,2048]{1,0:T(8,128)(2,1)S(1)} %slice.257), channel_id=1, source_target_pairs={{0,16},{8,24},{16,0},{24,8},{1,17},{9,25},{17,1},{25,9},{2,18},{10... | collective-permute-start | bytes 1572872 | tf_op jit(solution)/shard_map/ppermute | solution.py:93
  132.8 2.6 fusion.42
  135.5 1.3 slice.255
  136.8 2.1 collective-permute-start.9
  139.1 2.1 collective-permute-start.15
  141.2 2.4 fusion.19
  143.7 2.4 fusion.18
  146.2 1.4 collective-permute-start.16
  147.6 9.2 %collective-permute-done.5 = bf16[128,2048]{1,0:T(8,128)(2,1)S(1)} collective-permute-done((bf16[128,2048]{1,0:T(8,128)(2,1)S(1)}, bf16[128,2048]{1,0:T(8,128)(2,1)S(1)}, u32[]{:S(2)}, u32[]{:S(2)}) %collective-permute-start.5) | collective-permute-done | bytes 524320 | tf_op jit(solution)/shard_map/ppermute | solution.py:93
  156.8 0.8 copy-done.8
  157.6 2.0 collective-permute-start.21
  159.7 8.7 %convolution_convert_fusion.3 = bf16[128,4096]{1,0:T(8,128)(2,1)S(1)} fusion(bf16[2048,4096]{1,0:T(8,128)(2,1)} %param.11, f32[256,2048]{1,0:T(8,128)S(1)} %fusion.42, bf16[128,2048]{1,0:T(8,128)(2,1)} %copy-done.8, f32[256,2048]{1,0:T(8,128)S(1)} %fusion.43, bf16[128,2048]{1,0:T(8,128)(2,1)} %copy-done.7), kind=kOutput, calls=%fused_computation.3 | convolution fusion | flops 2150629376 | bytes 20971520 | tf_op jit(solution)/shard_map/dot_general | solution.py:132
  168.4 1.8 collective-permute-start.22
  170.2 9.2 %collective-permute-done.10 = bf16[128,2048]{1,0:T(8,128)(2,1)} collective-permute-done((bf16[128,2048]{1,0:T(8,128)(2,1)S(1)}, bf16[128,2048]{1,0:T(8,128)(2,1)}, u32[]{:S(2)}, u32[]{:S(2)}) %collective-permute-start.10) | collective-permute-done | bytes 524320 | tf_op jit(solution)/shard_map/ppermute | solution.py:93
  179.4 1.5 collective-permute-start.6
  180.9 8.7 %convolution_convert_fusion.2 = bf16[128,4096]{1,0:T(8,128)(2,1)S(1)} fusion(bf16[2048,4096]{1,0:T(8,128)(2,1)} %param.11, f32[256,2048]{1,0:T(8,128)S(1)} %copy-done.6, bf16[128,2048]{1,0:T(8,128)(2,1)} %collective-permute-done.10, f32[256,2048]{1,0:T(8,128)S(1)} %copy-done.4, bf16[128,2048]{1,0:T(8,128)(2,1)} %collective-permute-done.9), kind=kOutput, calls=%fused_computation.2 | convolution fusion | flops 2150629376 | bytes 20971520 | tf_op jit(solution)/shard_map/dot_general | solution.py:132
  189.7 0.9 collective-permute-done.15
  190.6 1.5 collective-permute-start.11
  192.1 9.6 %collective-permute-done.16 = bf16[128,2048]{1,0:T(8,128)(2,1)S(1)} collective-permute-done((bf16[128,2048]{1,0:T(8,128)(2,1)S(1)}, bf16[128,2048]{1,0:T(8,128)(2,1)S(1)}, u32[]{:S(2)}, u32[]{:S(2)}) %collective-permute-start.16) | collective-permute-done | bytes 524320 | tf_op jit(solution)/shard_map/ppermute | solution.py:93
  201.8 8.8 %convolution_convert_fusion.1 = bf16[128,4096]{1,0:T(8,128)(2,1)S(1)} fusion(bf16[2048,4096]{1,0:T(8,128)(2,1)} %param.11, f32[256,2048]{1,0:T(8,128)S(1)} %fusion.20, bf16[128,2048]{1,0:T(8,128)(2,1)S(1)} %collective-permute-done.16, f32[256,2048]{1,0:T(8,128)S(1)} %fusion.21, bf16[128,2048]{1,0:T(8,128)(2,1)} %collective-permute-done.15), kind=kOutput, calls=%fused_computation.1 | convolution fusion | flops 2150629376 | bytes 20971520 | tf_op jit(solution)/shard_map/dot_general | solution.py:132
  210.7 1.5 collective-permute-start.17
  212.6 5.6 %collective-permute-done.22 = bf16[128,2048]{1,0:T(8,128)(2,1)S(1)} collective-permute-done((bf16[128,2048]{1,0:T(8,128)(2,1)S(1)}, bf16[128,2048]{1,0:T(8,128)(2,1)S(1)}, u32[]{:S(2)}, u32[]{:S(2)}) %collective-permute-start.22) | collective-permute-done | bytes 524320 | tf_op jit(solution)/shard_map/ppermute | solution.py:93
  218.3 8.4 %convolution_convert_fusion = bf16[128,4096]{1,0:T(8,128)(2,1)S(1)} fusion(bf16[2048,4096]{1,0:T(8,128)(2,1)} %param.11, f32[256,2048]{1,0:T(8,128)S(1)} %fusion.18, bf16[128,2048]{1,0:T(8,128)(2,1)S(1)} %collective-permute-done.22, f32[256,2048]{1,0:T(8,128)S(1)} %fusion.19, bf16[128,2048]{1,0:T(8,128)(2,1)S(1)} %collective-permute-done.21), kind=kOutput, calls=%fused_computation | convolution fusion | flops 2150629376 | bytes 20971520 | tf_op jit(solution)/shard_map/dot_general | solution.py:132
  226.7 1.6 collective-permute-start.23
  228.4 3.4 %collective-permute-start.12 = (bf16[64,4096]{1,0:T(8,128)(2,1)S(1)}, bf16[64,4096]{1,0:T(8,128)(2,1)S(1)}, u32[]{:S(2)}, u32[]{:S(2)}) collective-permute-start(bf16[64,4096]{1,0:T(8,128)(2,1)S(1)} %add_convert_fusion.3), channel_id=1, source_target_pairs={{0,2},{1,3},{2,0},{3,1},{4,6},{5,7},{6,4},{7,5},{8,10},{9,11},{10,... | collective-permute-start | bytes 1572872 | tf_op jit(solution)/shard_map/ppermute | solution.py:93
  231.9 1.1 collective-permute-start.18
  233.1 2.9 %collective-permute-done.23 = bf16[64,4096]{1,0:T(8,128)(2,1)S(1)} collective-permute-done((bf16[64,4096]{1,0:T(8,128)(2,1)S(1)}, bf16[64,4096]{1,0:T(8,128)(2,1)S(1)}, u32[]{:S(2)}, u32[]{:S(2)}) %collective-permute-start.23) | collective-permute-done | bytes 524320 | tf_op jit(solution)/shard_map/ppermute | solution.py:93
  236.0 3.1 %collective-permute-start.24 = (bf16[64,4096]{1,0:T(8,128)(2,1)S(1)}, bf16[64,4096]{1,0:T(8,128)(2,1)S(1)}, u32[]{:S(2)}, u32[]{:S(2)}) collective-permute-start(bf16[64,4096]{1,0:T(8,128)(2,1)S(1)} %add_convert_fusion.1), channel_id=1, source_target_pairs={{0,6},{1,7},{2,4},{3,5},{4,2},{5,3},{6,0},{7,1},{8,14},{9,15},{10,... | collective-permute-start | bytes 1572872 | tf_op jit(solution)/shard_map/ppermute | solution.py:93
  239.2 9.0 %collective-permute-done.12 = bf16[64,4096]{1,0:T(8,128)(2,1)S(1)} collective-permute-done((bf16[64,4096]{1,0:T(8,128)(2,1)S(1)}, bf16[64,4096]{1,0:T(8,128)(2,1)S(1)}, u32[]{:S(2)}, u32[]{:S(2)}) %collective-permute-start.12) | collective-permute-done | bytes 524320 | tf_op jit(solution)/shard_map/ppermute | solution.py:93
  248.1 21.9 %collective-permute-done.18 = bf16[64,4096]{1,0:T(8,128)(2,1)S(1)} collective-permute-done((bf16[64,4096]{1,0:T(8,128)(2,1)S(1)}, bf16[64,4096]{1,0:T(8,128)(2,1)S(1)}, u32[]{:S(2)}, u32[]{:S(2)}) %collective-permute-start.18) | collective-permute-done | bytes 524320 | tf_op jit(solution)/shard_map/ppermute | solution.py:93
  270.1 1.2 add_convert_fusion
  (71 shorter events, 4.1 us)
Async XLA Ops:
  0.0 6.9 %copy-start = (bf16[1,1,128,4096]{3,2,1,0:T(8,128)(2,1)S(1)}, bf16[1,1,128,4096]{3,2,1,0:T(8,128)(2,1)}, u32[]{:S(2)}) copy-start(bf16[1,1,128,4096]{3,2,1,0:T(8,128)(2,1)} %param.6) | copy-start | bytes 3145732
  2.7 7.9 %all-to-all-start = ((s32[4,1,32]{2,1,0:T(1,128)}), s32[4,1,32]{2,1,0:T(1,128)S(1)}, u32[]{:S(2)}, u32[]{:S(2)}) async-start(s32[4,1,32]{2,1,0:T(1,128)} %bitcast.2), calls=%async_computation | async-start | bytes 4096 | tf_op jit(solution)/shard_map/all_to_all | solution.py:60
  10.6 18.0 %all-to-all-start.1 = ((bf16[4,32,4096]{2,1,0:T(8,128)(2,1)}), bf16[4,32,4096]{2,1,0:T(8,128)(2,1)S(1)}, u32[]{:S(2)}, u32[]{:S(2)}) async-start(bf16[4,32,4096]{2,1,0:T(8,128)(2,1)} %bitcast.4), calls=%async_computation.1 | async-start | bytes 2097152 | tf_op jit(solution)/shard_map/all_to_all | solution.py:53
  28.6 2.2 copy-start.2
  29.2 7.9 %collective-permute-start = (bf16[64,2048]{1,0:T(8,128)(2,1)S(1)}, bf16[64,2048]{1,0:T(8,128)(2,1)S(1)}, u32[]{:S(2)}, u32[]{:S(2)}) collective-permute-start(bf16[64,2048]{1,0:T(8,128)(2,1)S(1)} %pad_maximum_fusion.4), channel_id=1, source_target_pairs={{0,16},{8,24},{16,0},{24,8},{1,17},{9,25},{17,1},{25,9},{2,18},{10... | collective-permute-start | bytes 786440 | tf_op jit(solution)/shard_map/ppermute | solution.py:93
  30.7 72.7 %collective-permute-start.2 = (bf16[1024,2048]{1,0:T(8,128)(2,1)S(1)}, bf16[1024,2048]{1,0:T(8,128)(2,1)S(1)}, u32[]{:S(2)}, u32[]{:S(2)}) collective-permute-start(bf16[1024,2048]{1,0:T(8,128)(2,1)S(1)} %copy-done.2), channel_id=1, source_target_pairs={{0,8},{8,0},{16,24},{24,16},{1,9},{9,1},{17,25},{25,17},{2,10},{10... | collective-permute-start | bytes 12582920 | tf_op jit(solution)/shard_map/ppermute | solution.py:93
  30.7 82.2 %collective-permute-start.4 = (bf16[1024,2048]{1,0:T(8,128)(2,1)}, bf16[1024,2048]{1,0:T(8,128)(2,1)S(1)}, u32[]{:S(2)}, u32[]{:S(2)}) collective-permute-start(bf16[1024,2048]{1,0:T(8,128)(2,1)} %param.10), channel_id=1, source_target_pairs={{0,8},{8,0},{16,24},{24,16},{1,9},{9,1},{17,25},{25,17},{2,10},{10... | collective-permute-start | bytes 12582920 | tf_op jit(solution)/shard_map/ppermute | solution.py:93
  37.1 6.9 %copy-start.3 = (bf16[1024,2048]{1,0:T(8,128)(2,1)S(1)}, bf16[1024,2048]{1,0:T(8,128)(2,1)}, u32[]{:S(2)}) copy-start(bf16[1024,2048]{1,0:T(8,128)(2,1)} %param.10) | copy-start | bytes 12582916
  37.1 21.7 %collective-permute-start.7 = (bf16[128,2048]{1,0:T(8,128)(2,1)S(1)}, bf16[128,2048]{1,0:T(8,128)(2,1)S(1)}, u32[]{:S(2)}, u32[]{:S(2)}) collective-permute-start(bf16[128,2048]{1,0:T(8,128)(2,1)S(1)} %maximum_maximum_fusion), channel_id=1, source_target_pairs={{0,2},{1,3},{2,0},{3,1},{4,6},{5,7},{6,4},{7,5},{8,10},{9,11},{10,... | collective-permute-start | bytes 1572872 | tf_op jit(solution)/shard_map/ppermute | solution.py:93
  41.5 38.0 %collective-permute-start.13 = (bf16[128,2048]{1,0:T(8,128)(2,1)S(1)}, bf16[128,2048]{1,0:T(8,128)(2,1)S(1)}, u32[]{:S(2)}, u32[]{:S(2)}) collective-permute-start(bf16[128,2048]{1,0:T(8,128)(2,1)S(1)} %maximum_maximum_fusion), channel_id=1, source_target_pairs={{0,4},{1,5},{2,6},{3,7},{4,0},{5,1},{6,2},{7,3},{8,12},{9,13},{10,... | collective-permute-start | bytes 1572872 | tf_op jit(solution)/shard_map/ppermute | solution.py:93
  44.7 37.1 %collective-permute-start.1 = (bf16[128,2048]{1,0:T(8,128)(2,1)S(1)}, bf16[128,2048]{1,0:T(8,128)(2,1)S(1)}, u32[]{:S(2)}, u32[]{:S(2)}) collective-permute-start(bf16[128,2048]{1,0:T(8,128)(2,1)S(1)} %maximum_maximum_fusion), channel_id=1, source_target_pairs={{0,1},{1,0},{2,3},{3,2},{4,5},{5,4},{6,7},{7,6},{8,9},{9,8},{10,11... | collective-permute-start | bytes 1572872 | tf_op jit(solution)/shard_map/ppermute | solution.py:93
  58.9 22.2 %collective-permute-start.19 = (bf16[128,2048]{1,0:T(8,128)(2,1)S(1)}, bf16[128,2048]{1,0:T(8,128)(2,1)S(1)}, u32[]{:S(2)}, u32[]{:S(2)}) collective-permute-start(bf16[128,2048]{1,0:T(8,128)(2,1)S(1)} %maximum_maximum_fusion), channel_id=1, source_target_pairs={{0,6},{1,7},{2,4},{3,5},{4,2},{5,3},{6,0},{7,1},{8,14},{9,15},{10,... | collective-permute-start | bytes 1572872 | tf_op jit(solution)/shard_map/ppermute | solution.py:93
  79.5 12.6 %collective-permute-start.8 = (bf16[128,2048]{1,0:T(8,128)(2,1)S(1)}, bf16[128,2048]{1,0:T(8,128)(2,1)S(1)}, u32[]{:S(2)}, u32[]{:S(2)}) collective-permute-start(bf16[128,2048]{1,0:T(8,128)(2,1)S(1)} %collective-permute-done.7), channel_id=1, source_target_pairs={{0,1},{1,0},{2,3},{3,2},{4,5},{5,4},{6,7},{7,6},{8,9},{9,8},{10,11... | collective-permute-start | bytes 1572872 | tf_op jit(solution)/shard_map/ppermute | solution.py:93
  81.1 16.7 %collective-permute-start.14 = (bf16[128,2048]{1,0:T(8,128)(2,1)S(1)}, bf16[128,2048]{1,0:T(8,128)(2,1)S(1)}, u32[]{:S(2)}, u32[]{:S(2)}) collective-permute-start(bf16[128,2048]{1,0:T(8,128)(2,1)S(1)} %collective-permute-done.13), channel_id=1, source_target_pairs={{0,1},{1,0},{2,3},{3,2},{4,5},{5,4},{6,7},{7,6},{8,9},{9,8},{10,11... | collective-permute-start | bytes 1572872 | tf_op jit(solution)/shard_map/ppermute | solution.py:93
  81.7 21.7 %collective-permute-start.20 = (bf16[128,2048]{1,0:T(8,128)(2,1)S(1)}, bf16[128,2048]{1,0:T(8,128)(2,1)S(1)}, u32[]{:S(2)}, u32[]{:S(2)}) collective-permute-start(bf16[128,2048]{1,0:T(8,128)(2,1)S(1)} %collective-permute-done.19), channel_id=1, source_target_pairs={{0,1},{1,0},{2,3},{3,2},{4,5},{5,4},{6,7},{7,6},{8,9},{9,8},{10,11... | collective-permute-start | bytes 1572872 | tf_op jit(solution)/shard_map/ppermute | solution.py:93
  112.9 3.0 %slice-start = ((s8[8388608]{0:T(1024)(128)(4,1)}), s8[4194304]{0:T(1024)(128)(4,1)S(1)}, s32[]{:S(2)}) async-start(s8[8388608]{0:T(1024)(128)(4,1)} %bitcast.37), calls=%async_computation.2 | async-start | bytes 8388608
  113.5 3.0 %slice-start.1 = ((s8[8388608]{0:T(1024)(128)(4,1)}), s8[4194304]{0:T(1024)(128)(4,1)S(1)}, s32[]{:S(2)}) async-start(s8[8388608]{0:T(1024)(128)(4,1)} %bitcast.37), calls=%async_computation.3 | async-start | bytes 8388608
  115.9 23.0 %copy-start.5 = (f32[256,2048]{1,0:T(8,128)}, f32[256,2048]{1,0:T(8,128)S(1)}, u32[]{:S(2)}) copy-start(f32[256,2048]{1,0:T(8,128)S(1)} %fusion.22) | copy-start | bytes 6291460
  123.8 22.4 %collective-permute-start.3 = (bf16[128,2048]{1,0:T(8,128)(2,1)S(1)}, bf16[128,2048]{1,0:T(8,128)(2,1)S(1)}, u32[]{:S(2)}, u32[]{:S(2)}) collective-permute-start(bf16[128,2048]{1,0:T(8,128)(2,1)S(1)} %slice.257), channel_id=1, source_target_pairs={{0,16},{8,24},{16,0},{24,8},{1,17},{9,25},{17,1},{25,9},{2,18},{10... | collective-permute-start | bytes 1572872 | tf_op jit(solution)/shard_map/ppermute | solution.py:93
  135.4 21.4 %collective-permute-start.5 = (bf16[128,2048]{1,0:T(8,128)(2,1)S(1)}, bf16[128,2048]{1,0:T(8,128)(2,1)S(1)}, u32[]{:S(2)}, u32[]{:S(2)}) collective-permute-start(bf16[128,2048]{1,0:T(8,128)(2,1)S(1)} %slice.256), channel_id=1, source_target_pairs={{0,16},{8,24},{16,0},{24,8},{1,17},{9,25},{17,1},{25,9},{2,18},{10... | collective-permute-start | bytes 1572872 | tf_op jit(solution)/shard_map/ppermute | solution.py:93
  136.8 31.6 %collective-permute-start.9 = (bf16[128,2048]{1,0:T(8,128)(2,1)S(1)}, bf16[128,2048]{1,0:T(8,128)(2,1)}, u32[]{:S(2)}, u32[]{:S(2)}) collective-permute-start(bf16[128,2048]{1,0:T(8,128)(2,1)S(1)} %slice.255), channel_id=1, source_target_pairs={{0,16},{8,24},{16,0},{24,8},{1,17},{9,25},{17,1},{25,9},{2,18},{10... | collective-permute-start | bytes 1572872 | tf_op jit(solution)/shard_map/ppermute | solution.py:93
  139.0 40.5 %collective-permute-start.10 = (bf16[128,2048]{1,0:T(8,128)(2,1)S(1)}, bf16[128,2048]{1,0:T(8,128)(2,1)}, u32[]{:S(2)}, u32[]{:S(2)}) collective-permute-start(bf16[128,2048]{1,0:T(8,128)(2,1)S(1)} %slice.254), channel_id=1, source_target_pairs={{0,16},{8,24},{16,0},{24,8},{1,17},{9,25},{17,1},{25,9},{2,18},{10... | collective-permute-start | bytes 1572872 | tf_op jit(solution)/shard_map/ppermute | solution.py:93
  139.1 51.5 %collective-permute-start.15 = (bf16[128,2048]{1,0:T(8,128)(2,1)S(1)}, bf16[128,2048]{1,0:T(8,128)(2,1)}, u32[]{:S(2)}, u32[]{:S(2)}) collective-permute-start(bf16[128,2048]{1,0:T(8,128)(2,1)S(1)} %slice.253), channel_id=1, source_target_pairs={{0,16},{8,24},{16,0},{24,8},{1,17},{9,25},{17,1},{25,9},{2,18},{10... | collective-permute-start | bytes 1572872 | tf_op jit(solution)/shard_map/ppermute | solution.py:93
  146.2 34.7 %copy-start.4 = (f32[256,2048]{1,0:T(8,128)S(1)}, f32[256,2048]{1,0:T(8,128)}, u32[]{:S(2)}) copy-start(f32[256,2048]{1,0:T(8,128)} %fusion.23) | copy-start | bytes 6291460
  146.2 34.7 %copy-start.6 = (f32[256,2048]{1,0:T(8,128)S(1)}, f32[256,2048]{1,0:T(8,128)}, u32[]{:S(2)}) copy-start(f32[256,2048]{1,0:T(8,128)} %copy-done.5) | copy-start | bytes 6291460
  146.2 10.6 %copy-start.7 = (bf16[128,2048]{1,0:T(8,128)(2,1)}, bf16[128,2048]{1,0:T(8,128)(2,1)S(1)}, u32[]{:S(2)}) copy-start(bf16[128,2048]{1,0:T(8,128)(2,1)S(1)} %collective-permute-done.3) | copy-start | bytes 1572868
  146.2 55.5 %collective-permute-start.16 = (bf16[128,2048]{1,0:T(8,128)(2,1)S(1)}, bf16[128,2048]{1,0:T(8,128)(2,1)S(1)}, u32[]{:S(2)}, u32[]{:S(2)}) collective-permute-start(bf16[128,2048]{1,0:T(8,128)(2,1)S(1)} %slice.252), channel_id=1, source_target_pairs={{0,16},{8,24},{16,0},{24,8},{1,17},{9,25},{17,1},{25,9},{2,18},{10... | collective-permute-start | bytes 1572872 | tf_op jit(solution)/shard_map/ppermute | solution.py:93
  156.8 0.8 copy-start.8
  157.6 55.0 %collective-permute-start.21 = (bf16[128,2048]{1,0:T(8,128)(2,1)S(1)}, bf16[128,2048]{1,0:T(8,128)(2,1)S(1)}, u32[]{:S(2)}, u32[]{:S(2)}) collective-permute-start(bf16[128,2048]{1,0:T(8,128)(2,1)S(1)} %slice.251), channel_id=1, source_target_pairs={{0,16},{8,24},{16,0},{24,8},{1,17},{9,25},{17,1},{25,9},{2,18},{10... | collective-permute-start | bytes 1572872 | tf_op jit(solution)/shard_map/ppermute | solution.py:93
  168.4 49.8 %collective-permute-start.22 = (bf16[128,2048]{1,0:T(8,128)(2,1)S(1)}, bf16[128,2048]{1,0:T(8,128)(2,1)S(1)}, u32[]{:S(2)}, u32[]{:S(2)}) collective-permute-start(bf16[128,2048]{1,0:T(8,128)(2,1)S(1)} %slice.250), channel_id=1, source_target_pairs={{0,16},{8,24},{16,0},{24,8},{1,17},{9,25},{17,1},{25,9},{2,18},{10... | collective-permute-start | bytes 1572872 | tf_op jit(solution)/shard_map/ppermute | solution.py:93
  179.4 59.8 %collective-permute-start.6 = (bf16[64,4096]{1,0:T(8,128)(2,1)S(1)}, bf16[64,4096]{1,0:T(8,128)(2,1)S(1)}, u32[]{:S(2)}, u32[]{:S(2)}) collective-permute-start(bf16[64,4096]{1,0:T(8,128)(2,1)S(1)} %slice.167), channel_id=1, source_target_pairs={{0,1},{1,0},{2,3},{3,2},{4,5},{5,4},{6,7},{7,6},{8,9},{9,8},{10,11... | collective-permute-start | bytes 1572872 | tf_op jit(solution)/shard_map/ppermute | solution.py:93
  190.6 37.6 %collective-permute-start.11 = (bf16[64,4096]{1,0:T(8,128)(2,1)S(1)}, bf16[64,4096]{1,0:T(8,128)(2,1)S(1)}, u32[]{:S(2)}, u32[]{:S(2)}) collective-permute-start(bf16[64,4096]{1,0:T(8,128)(2,1)S(1)} %slice.177), channel_id=1, source_target_pairs={{0,1},{1,0},{2,3},{3,2},{4,5},{5,4},{6,7},{7,6},{8,9},{9,8},{10,11... | collective-permute-start | bytes 1572872 | tf_op jit(solution)/shard_map/ppermute | solution.py:93
  210.7 21.1 %collective-permute-start.17 = (bf16[64,4096]{1,0:T(8,128)(2,1)S(1)}, bf16[64,4096]{1,0:T(8,128)(2,1)S(1)}, u32[]{:S(2)}, u32[]{:S(2)}) collective-permute-start(bf16[64,4096]{1,0:T(8,128)(2,1)S(1)} %slice.187), channel_id=1, source_target_pairs={{0,1},{1,0},{2,3},{3,2},{4,5},{5,4},{6,7},{7,6},{8,9},{9,8},{10,11... | collective-permute-start | bytes 1572872 | tf_op jit(solution)/shard_map/ppermute | solution.py:93
  226.7 9.2 %collective-permute-start.23 = (bf16[64,4096]{1,0:T(8,128)(2,1)S(1)}, bf16[64,4096]{1,0:T(8,128)(2,1)S(1)}, u32[]{:S(2)}, u32[]{:S(2)}) collective-permute-start(bf16[64,4096]{1,0:T(8,128)(2,1)S(1)} %slice.197), channel_id=1, source_target_pairs={{0,1},{1,0},{2,3},{3,2},{4,5},{5,4},{6,7},{7,6},{8,9},{9,8},{10,11... | collective-permute-start | bytes 1572872 | tf_op jit(solution)/shard_map/ppermute | solution.py:93
  228.4 19.8 %collective-permute-start.12 = (bf16[64,4096]{1,0:T(8,128)(2,1)S(1)}, bf16[64,4096]{1,0:T(8,128)(2,1)S(1)}, u32[]{:S(2)}, u32[]{:S(2)}) collective-permute-start(bf16[64,4096]{1,0:T(8,128)(2,1)S(1)} %add_convert_fusion.3), channel_id=1, source_target_pairs={{0,2},{1,3},{2,0},{3,1},{4,6},{5,7},{6,4},{7,5},{8,10},{9,11},{10,... | collective-permute-start | bytes 1572872 | tf_op jit(solution)/shard_map/ppermute | solution.py:93
  231.9 38.1 %collective-permute-start.18 = (bf16[64,4096]{1,0:T(8,128)(2,1)S(1)}, bf16[64,4096]{1,0:T(8,128)(2,1)S(1)}, u32[]{:S(2)}, u32[]{:S(2)}) collective-permute-start(bf16[64,4096]{1,0:T(8,128)(2,1)S(1)} %add_convert_fusion.2), channel_id=1, source_target_pairs={{0,4},{1,5},{2,6},{3,7},{4,0},{5,1},{6,2},{7,3},{8,12},{9,13},{10,... | collective-permute-start | bytes 1572872 | tf_op jit(solution)/shard_map/ppermute | solution.py:93
  235.9 35.4 %copy-start.1 = (bf16[1,1,128,4096]{3,2,1,0:T(8,128)(2,1)S(1)}, bf16[1,1,128,4096]{3,2,1,0:T(8,128)(2,1)}, u32[]{:S(2)}) copy-start(bf16[1,1,128,4096]{3,2,1,0:T(8,128)(2,1)} %param.6) | copy-start | bytes 3145732
  236.0 34.0 %collective-permute-start.24 = (bf16[64,4096]{1,0:T(8,128)(2,1)S(1)}, bf16[64,4096]{1,0:T(8,128)(2,1)S(1)}, u32[]{:S(2)}, u32[]{:S(2)}) collective-permute-start(bf16[64,4096]{1,0:T(8,128)(2,1)S(1)} %add_convert_fusion.1), channel_id=1, source_target_pairs={{0,6},{1,7},{2,4},{3,5},{4,2},{5,3},{6,0},{7,1},{8,14},{9,15},{10,... | collective-permute-start | bytes 1572872 | tf_op jit(solution)/shard_map/ppermute | solution.py:93

commit v2 on v0

--- a/solution.py
+++ b/solution.py
@@ -1,9 +1,14 @@
+import functools
+
 import jax
 import jax.numpy as jnp
 from jax import lax
+from jax.experimental import pallas as pl
+from jax.experimental.pallas import tpu as pltpu
 from jax.sharding import PartitionSpec as P
 
 ROWS_GRP = 512
+MESH = pl.DeviceIdType.MESH
 
 
 def swiglu(inputs, gate_full, up_full):
@@ -24,7 +29,7 @@
     return lax.optimization_barrier(partial_sum.astype(jnp.bfloat16)).astype(jnp.float32)
 
 
-def per_device(loader_rows, row_counts, row_targets, gate_weight, up_weight, down_weight):
+def rebalance(loader_rows, row_counts, row_targets):
     dp_count = lax.axis_size("dp")
     tp_count = lax.axis_size("tensor")
     slot_rows = loader_rows[0, 0]
@@ -68,6 +73,11 @@
     local_batch = jnp.dot(
         land_matrix, arrived.reshape(slot_count, feature_count), preferred_element_type=jnp.float32
     ).astype(jnp.bfloat16)
+    return local_batch
+
+
+def gathered_plan(loader_rows, row_counts, row_targets, gate_weight, up_weight, down_weight):
+    local_batch = rebalance(loader_rows, row_counts, row_targets)
     gate_full, up_full = (
         lax.all_gather(gate_weight, "dp", axis=0, tiled=True),
         lax.all_gather(up_weight, "dp", axis=0, tiled=True),
@@ -83,6 +93,224 @@
     return (local_batch.astype(jnp.float32) + summed).astype(jnp.bfloat16)
 
 
+def ff_kernel(
+    order, norm_ref, batch_ref, gate_ref, up_ref, down_ref, out_ref,
+    gate_v, up_v, down_v, rows_v, part_out, part_in, hidden_v, term_v, x_in, z_in,
+    local_sem, send_sem, recv_sem,
+):
+    me = lax.axis_index("dp")
+    place = lax.axis_index("tensor")
+    core, y = lax.rem(me, 2), lax.div(me, 2)
+    x, z = lax.rem(place, 2), lax.div(place, 2)
+    core_peer = {"dp": 2 * y + 1 - core}
+    y_peer = {"dp": 2 * (1 - y) + core}
+    x_peer = {"tensor": 2 * z + 1 - x}
+    z_peer = {
+        1: {"tensor": 2 * (z + 1 - 2 * lax.rem(z, 2)) + x},
+        2: {"tensor": 2 * lax.rem(z + 2, 4) + x},
+        3: {"tensor": 2 * (3 - z) + x},
+    }
+    shard_rows = norm_ref.shape[0]
+    half = norm_ref.shape[1] // 2
+    width = gate_ref.shape[0]
+    hidden_width = gate_ref.shape[1]
+    tile = 512
+
+    barrier = pltpu.get_barrier_semaphore()
+    for peer in (core_peer, y_peer, x_peer, z_peer[1], z_peer[2], z_peer[3]):
+        pl.semaphore_signal(barrier, inc=1, device_id=peer, device_id_type=MESH)
+    pl.semaphore_wait(barrier, 6)
+
+    def send(index, src, dst, peer):
+        copy = pltpu.make_async_remote_copy(
+            src_ref=src,
+            dst_ref=dst,
+            send_sem=send_sem.at[index],
+            recv_sem=recv_sem.at[index],
+            device_id=peer,
+            device_id_type=MESH,
+        )
+        copy.start()
+        sent.append(copy)
+        return copy
+
+    sent = []
+    own_cols = pl.ds(pl.multiple_of(y * half, half), half)
+    peer_cols = pl.ds(pl.multiple_of((1 - y) * half, half), half)
+    own_block = pl.ds(pl.multiple_of(core * width, width), width)
+    first = send(
+        0, norm_ref.at[:, peer_cols], rows_v.at[0, 0, pl.ds(0, shard_rows), :], y_peer
+    )
+    own_rows = pltpu.make_async_copy(
+        norm_ref.at[:, own_cols], rows_v.at[0, 1, pl.ds(0, shard_rows), :], local_sem.at[0]
+    )
+    own_rows.start()
+    gate_swap = send(1, gate_ref, gate_v.at[own_block, :], core_peer)
+    gate_own = pltpu.make_async_copy(gate_ref, gate_v.at[own_block, :], local_sem.at[1])
+    gate_own.start()
+    up_swap = send(2, up_ref, up_v.at[own_block, :], core_peer)
+    up_own = pltpu.make_async_copy(up_ref, up_v.at[own_block, :], local_sem.at[2])
+    up_own.start()
+    down_own = pltpu.make_async_copy(down_ref, down_v, local_sem.at[3])
+    down_own.start()
+
+    near = pl.ds(0, shard_rows)
+    far = pl.ds(shard_rows, shard_rows)
+    own_rows.wait()
+    first.wait_recv()
+    z_copy, x_copy = {}, {}
+
+    def spread(step):
+        z_copy[step] = send(
+            2 + step, rows_v.at[0, :, near, :], rows_v.at[step, :, near, :], z_peer[step]
+        )
+
+    def cross(step):
+        if step:
+            z_copy[step].wait_recv()
+        x_copy[step] = send(
+            6 + step, rows_v.at[step, :, near, :], rows_v.at[step, :, far, :], x_peer
+        )
+
+    parts = {}
+
+    def project(step):
+        x_copy[step].wait_recv()
+        for which, weight in ((0, gate_v), (1, up_v)):
+            if step == order[0]:
+                (gate_swap, up_swap)[which].wait_recv()
+                (gate_own, up_own)[which].wait()
+
+            def body(i, carry):
+                cols = pl.ds(pl.multiple_of(i * tile, tile), tile)
+                part_out[step, which, :, cols] = jnp.dot(
+                    rows_v[step, 0], weight[:, cols], preferred_element_type=jnp.float32
+                ).astype(jnp.bfloat16)
+                return carry
+
+            lax.fori_loop(0, hidden_width // tile, body, 0)
+            parts[step, which] = send(
+                10 + 2 * step + which, part_out.at[step, which], part_in.at[step, which], y_peer
+            )
+
+    term_copy, pair_copy = {}, {}
+
+    def finish(step):
+        parts[step, 0].wait_recv()
+        parts[step, 1].wait_recv()
+
+        def body(i, carry):
+            cols = pl.ds(pl.multiple_of(i * tile, tile), tile)
+            rows = rows_v[step, 1]
+            gate_sum = jnp.dot(
+                rows, gate_v[:, cols], preferred_element_type=jnp.float32
+            ) + part_in[step, 0, :, cols].astype(jnp.float32)
+            up_sum = jnp.dot(
+                rows, up_v[:, cols], preferred_element_type=jnp.float32
+            ) + part_in[step, 1, :, cols].astype(jnp.float32)
+            hidden_v[:, cols] = (gate_sum / (1.0 + jnp.exp(-gate_sum)) * up_sum).astype(
+                jnp.bfloat16
+            )
+            return carry
+
+        lax.fori_loop(0, hidden_width // tile, body, 0)
+        if step == order[0]:
+            down_own.wait()
+
+        def down_body(i, carry):
+            cols = pl.ds(pl.multiple_of(i * tile, tile), tile)
+            term_v[step, :, cols] = jnp.dot(
+                hidden_v[...], down_v[:, cols], preferred_element_type=jnp.float32
+            ).astype(jnp.bfloat16)
+            return carry
+
+        lax.fori_loop(0, 2 * half // tile, down_body, 0)
+        term_copy[step] = send(18 + step, term_v.at[step, far, :], x_in.at[step], x_peer)
+
+    def pair(step):
+        term_copy[step].wait_recv()
+        term_v[step, near, :] = (
+            term_v[step, near, :].astype(jnp.float32) + x_in[step].astype(jnp.float32)
+        ).astype(jnp.bfloat16)
+        pair_copy[step] = send(21 + step, term_v.at[step, near, :], z_in.at[step - 1], z_peer[step])
+
+    s0, s1, s2, s3 = order
+    cross(s0)
+    spread(s1)
+    project(s0)
+    spread(s2)
+    cross(s1)
+    project(s1)
+    spread(s3)
+    cross(s2)
+    finish(s0)
+    project(s2)
+    cross(s3)
+    finish(s1)
+    project(s3)
+    pair(s1)
+    finish(s2)
+    pair(s2)
+    finish(s3)
+    pair(s3)
+    term_copy[0].wait_recv()
+    total = (
+        batch_ref[...].astype(jnp.float32)
+        + term_v[0, near, :].astype(jnp.float32)
+        + x_in[0].astype(jnp.float32)
+    )
+    for step in (s1, s2, s3):
+        pair_copy[step].wait_recv()
+        total = total + z_in[step - 1].astype(jnp.float32)
+    out_ref[...] = total.astype(jnp.bfloat16)
+    for copy in sent:
+        copy.wait_send()
+
+
+def chip_plan(loader_rows, row_counts, row_targets, gate_weight, up_weight, down_weight):
+    local_batch = rebalance(loader_rows, row_counts, row_targets)
+    travelling = normalize(local_batch)
+    shard_rows, features = local_batch.shape
+    hidden_width = gate_weight.shape[1]
+    half = features // 2
+    vmem = pl.BlockSpec(memory_space=pltpu.VMEM)
+    any_space = pl.BlockSpec(memory_space=pl.ANY)
+    bf16 = jnp.bfloat16
+    return pl.pallas_call(
+        functools.partial(ff_kernel, (0, 2, 3, 1)),
+        out_shape=jax.ShapeDtypeStruct((shard_rows, features), bf16),
+        in_specs=[vmem, vmem, any_space, any_space, any_space],
+        out_specs=vmem,
+        scratch_shapes=[
+            pltpu.VMEM((half, hidden_width), bf16),
+            pltpu.VMEM((half, hidden_width), bf16),
+            pltpu.VMEM((hidden_width, features), bf16),
+            pltpu.VMEM((4, 2, 2 * shard_rows, half), bf16),
+            pltpu.VMEM((4, 2, 2 * shard_rows, hidden_width), bf16),
+            pltpu.VMEM((4, 2, 2 * shard_rows, hidden_width), bf16),
+            pltpu.VMEM((2 * shard_rows, hidden_width), bf16),
+            pltpu.VMEM((4, 2 * shard_rows, features), bf16),
+            pltpu.VMEM((4, shard_rows, features), bf16),
+            pltpu.VMEM((3, shard_rows, features), bf16),
+            pltpu.SemaphoreType.DMA((4,)),
+            pltpu.SemaphoreType.DMA((25,)),
+            pltpu.SemaphoreType.DMA((25,)),
+        ],
+        compiler_params=pltpu.CompilerParams(
+            collective_id=0, has_side_effects=True, vmem_limit_bytes=60 * 1024 * 1024
+        ),
+        cost_estimate=pl.CostEstimate(
+            flops=26 * 10**9, bytes_accessed=26 * 2**20, transcendentals=2**20
+        ),
+    )(travelling, local_batch, gate_weight, up_weight, down_weight)
+
+
+def per_device(*args):
+    if lax.axis_size("dp") == 4 and lax.axis_size("tensor") == 8:
+        return chip_plan(*args)
+    return gathered_plan(*args)
+
+
 def solution(mesh):
     placed = (
         P("dp", "tensor", None, None),

time: 452 us -> 185 us (0.41)
  waiting for transfers between devices: 376 us -> 15.4 us
  Pallas kernels: 0 us -> 152 us
  matrix products: 48.2 us -> 1.81 us
  between operations: 13.8 us -> 0.81 us
    all_gather x3 -> x0, waiting for transfers between devices: 271 us -> none  [the longest x1 106 us: per_device(): lax.all_gather(gate_weight, 'dp', axis=0, tiled=True)]
    pallas_call x0 -> x1, Pallas kernels: none -> 152 us  [chip_plan(): pl.pallas_call(functools.partial(ff_kernel, (0, 2, 3, 1)), out_shape=jax....]
    reduce_scatter x1 -> x0, waiting for transfers between devices: 88 us -> none  [per_device(): lax.psum_scatter(rounded_term(hidden, down_weight).astype(jnp.bfloat16),...]
    dot_general x4 -> x2, matrix products: 48.2 us -> 1.81 us  [the longest x1 1.42 us: rebalance(): jnp.dot(pick_matrix.astype(jnp.bfloat16), slot_rows, preferred_element_ty...]
  transfers between devices with their start and end apart: 6 -> 2, of which waited for: 6 -> 2; matrix products, arithmetic and copies ran while one was open for 4% -> 1% of each run, Pallas kernels for 0% -> 0%
where the time goes in v2:
time: 185 us; the launch traced here: 184 us
  Pallas kernels  152 us (82%)
  waiting for transfers between devices  15.4 us (8%)
  starting transfers between devices  7.75 us (4%)
  local copies, waits for them, and re-layouts  3.14 us (2%)
  other arithmetic  2.87 us (2%)
    pallas_call x1, Pallas kernels, chip_plan(): pl.pallas_call(functools.partial(ff_kernel, (0, 2, 3, 1)), out_shape=jax....  152 us
    all_to_all x1, waiting for transfers between devices, rebalance(): lax.all_to_all(outgoing.reshape(dp_count, per_peer, feature_count), 'dp',...  13.2 us
    all_to_all x1, starting transfers between devices, rebalance(): lax.all_to_all(out_place.reshape(dp_count, per_peer), 'dp', split_axis=0,...  4.24 us
  transfers between devices with their start and end apart: 2, of which 2 were waited for; matrix products, arithmetic and copies ran while one was open for 1% of the time, Pallas kernels for 0%

profile of v2, /device:TPU:0, one launch (start us, length us, event | category | flops | bytes accessed | tf_op | source)
XLA Modules:
  0.0 183.8 jit_solution(7891265862357347182)
XLA Ops:
  0.0 0.0 copy-start
  0.8 0.7 fusion.10
  1.4 0.1 fusion.4
  1.5 0.2 reduce_window_sum.11
  1.7 0.2 select_reduce_fusion.1
  1.9 0.1 select_reduce_fusion
  2.0 0.7 sub.18
  2.7 4.2 %all-to-all-start = ((s32[4,1,32]{2,1,0:T(1,128)}), s32[4,1,32]{2,1,0:T(1,128)S(1)}, u32[]{:S(2)}, u32[]{:S(2)}) async-start(s32[4,1,32]{2,1,0:T(1,128)} %bitcast.2), calls=%async_computation | async-start | bytes 4096 | tf_op jit(solution)/shard_map/all_to_all | solution.py:65
  6.9 0.0 copy-done
  6.9 1.4 convolution_convert_fusion
  8.3 2.3 %all-to-all-done = s32[4,1,32]{2,1,0:T(1,128)S(1)} async-done(((s32[4,1,32]{2,1,0:T(1,128)}), s32[4,1,32]{2,1,0:T(1,128)S(1)}, u32[]{:S(2)}, u32[]{:S(2)}) %all-to-all-start) | async-done | bytes 544 | tf_op jit(solution)/shard_map/all_to_all | solution.py:65
  10.6 3.5 %all-to-all-start.1 = ((bf16[4,32,4096]{2,1,0:T(8,128)(2,1)}), bf16[4,32,4096]{2,1,0:T(8,128)(2,1)S(1)}, u32[]{:S(2)}, u32[]{:S(2)}) async-start(bf16[4,32,4096]{2,1,0:T(8,128)(2,1)} %bitcast.4), calls=%async_computation.1 | async-start | bytes 2097152 | tf_op jit(solution)/shard_map/all_to_all | solution.py:58
  14.1 0.5 broadcast.145
  14.6 0.7 reduce.3
  15.3 0.1 eq.49
  15.4 13.2 %all-to-all-done.1 = bf16[4,32,4096]{2,1,0:T(8,128)(2,1)S(1)} async-done(((bf16[4,32,4096]{2,1,0:T(8,128)(2,1)}), bf16[4,32,4096]{2,1,0:T(8,128)(2,1)S(1)}, u32[]{:S(2)}, u32[]{:S(2)}) %all-to-all-start.1) | async-done | bytes 1048608 | tf_op jit(solution)/shard_map/all_to_all | solution.py:58
  28.6 0.4 fusion
  28.9 0.0 copy-start.1
  29.0 1.0 fusion.1.norm_ref
  29.9 0.0 copy-done.1
  29.9 152.0 %shard_map.64 = bf16[64,4096]{1,0:T(8,128)(2,1)} custom-call(bf16[64,4096]{1,0:T(8,128)(2,1)} %fusion.1.norm_ref, bf16[64,4096]{1,0:T(8,128)(2,1)} %copy-done.1, bf16[1024,2048]{1,0:T(8,128)(2,1)} %gate_ref.1, bf16[1024,2048]{1,0:T(8,128)(2,1)} %up_ref.1, bf16[2048,4096]{1,0:T(8,128)(2,1)} %down_ref.1), custom_call_target="tpu_custom_call" | custom-call | flops 25999998976 | bytes 27262976 | tf_op jit(solution)/shard_map/pallas_call | solution.py:279
  181.9 1.9 %copy.11 = bf16[64,4096]{1,0:T(8,128)(2,1)} copy(bf16[64,4096]{1,0:T(8,128)(2,1)} %shard_map.64) | data formatting | bytes 1048576
  (4 shorter events, 0.0 us)
Async XLA Ops:
  0.0 6.9 %copy-start = (bf16[1,1,128,4096]{3,2,1,0:T(8,128)(2,1)S(1)}, bf16[1,1,128,4096]{3,2,1,0:T(8,128)(2,1)}, u32[]{:S(2)}) copy-start(bf16[1,1,128,4096]{3,2,1,0:T(8,128)(2,1)} %param.6) | copy-start | bytes 3145732
  2.7 7.9 %all-to-all-start = ((s32[4,1,32]{2,1,0:T(1,128)}), s32[4,1,32]{2,1,0:T(1,128)S(1)}, u32[]{:S(2)}, u32[]{:S(2)}) async-start(s32[4,1,32]{2,1,0:T(1,128)} %bitcast.2), calls=%async_computation | async-start | bytes 4096 | tf_op jit(solution)/shard_map/all_to_all | solution.py:65
  10.6 18.0 %all-to-all-start.1 = ((bf16[4,32,4096]{2,1,0:T(8,128)(2,1)}), bf16[4,32,4096]{2,1,0:T(8,128)(2,1)S(1)}, u32[]{:S(2)}, u32[]{:S(2)}) async-start(bf16[4,32,4096]{2,1,0:T(8,128)(2,1)} %bitcast.4), calls=%async_computation.1 | async-start | bytes 2097152 | tf_op jit(solution)/shard_map/all_to_all | solution.py:58
  28.9 1.0 copy-start.1

commit v3 on v2

--- a/solution.py
+++ b/solution.py
@@ -1,5 +1,3 @@
-import functools
-
 import jax
 import jax.numpy as jnp
 from jax import lax
@@ -29,7 +27,7 @@
     return lax.optimization_barrier(partial_sum.astype(jnp.bfloat16)).astype(jnp.float32)
 
 
-def rebalance(loader_rows, row_counts, row_targets):
+def pick_slots(loader_rows, row_counts, row_targets):
     dp_count = lax.axis_size("dp")
     tp_count = lax.axis_size("tensor")
     slot_rows = loader_rows[0, 0]
@@ -50,6 +48,14 @@
     slot_rank = jnp.sum(earlier * peer_hot, axis=1)
     send_slot = peer_index * per_peer + slot_rank
     pick_matrix = (send_slot[None, :] == slot_index[:, None]) & is_live[None, :]
+    return pick_matrix, slot_rows, row_place, is_live, dp_count, per_peer, shard_rows
+
+
+def rebalance(loader_rows, row_counts, row_targets):
+    pick_matrix, slot_rows, row_place, is_live, dp_count, per_peer, shard_rows = pick_slots(
+        loader_rows, row_counts, row_targets
+    )
+    slot_count, feature_count = slot_rows.shape
     outgoing = jnp.dot(
         pick_matrix.astype(jnp.bfloat16), slot_rows, preferred_element_type=jnp.float32
     ).astype(jnp.bfloat16)
@@ -94,8 +100,8 @@
 
 
 def ff_kernel(
-    order, norm_ref, batch_ref, gate_ref, up_ref, down_ref, out_ref,
-    gate_v, up_v, down_v, rows_v, part_out, part_in, hidden_v, term_v, x_in, z_in,
+    leaving_ref, leaving_place_ref, gate_ref, up_ref, down_ref, out_ref,
+    arrived_v, place_v, batch_v, norm_v, gate_v, up_v, down_v, rows_v, part_out, part_in, hidden_v, term_v, x_in, z_in,
     local_sem, send_sem, recv_sem,
 ):
     me = lax.axis_index("dp")
@@ -104,24 +110,29 @@
     x, z = lax.rem(place, 2), lax.div(place, 2)
     core_peer = {"dp": 2 * y + 1 - core}
     y_peer = {"dp": 2 * (1 - y) + core}
+    corner_peer = {"dp": 2 * (1 - y) + 1 - core}
     x_peer = {"tensor": 2 * z + 1 - x}
     z_peer = {
         1: {"tensor": 2 * (z + 1 - 2 * lax.rem(z, 2)) + x},
         2: {"tensor": 2 * lax.rem(z + 2, 4) + x},
         3: {"tensor": 2 * (3 - z) + x},
     }
-    shard_rows = norm_ref.shape[0]
-    half = norm_ref.shape[1] // 2
+    shard_rows, features = batch_v.shape
+    half = features // 2
+    per_peer = arrived_v.shape[1]
     width = gate_ref.shape[0]
     hidden_width = gate_ref.shape[1]
     tile = 512
 
     barrier = pltpu.get_barrier_semaphore()
-    for peer in (core_peer, y_peer, x_peer, z_peer[1], z_peer[2], z_peer[3]):
+    for peer in (core_peer, y_peer, corner_peer, x_peer, z_peer[1], z_peer[2], z_peer[3]):
         pl.semaphore_signal(barrier, inc=1, device_id=peer, device_id_type=MESH)
-    pl.semaphore_wait(barrier, 6)
-
-    def send(index, src, dst, peer):
+    pl.semaphore_wait(barrier, 7)
+
+    sent = []
+
+    def send(src, dst, peer):
+        index = len(sent)
         copy = pltpu.make_async_remote_copy(
             src_ref=src,
             dst_ref=dst,
@@ -134,25 +145,55 @@
         sent.append(copy)
         return copy
 
-    sent = []
     own_cols = pl.ds(pl.multiple_of(y * half, half), half)
     peer_cols = pl.ds(pl.multiple_of((1 - y) * half, half), half)
     own_block = pl.ds(pl.multiple_of(core * width, width), width)
-    first = send(
-        0, norm_ref.at[:, peer_cols], rows_v.at[0, 0, pl.ds(0, shard_rows), :], y_peer
-    )
-    own_rows = pltpu.make_async_copy(
-        norm_ref.at[:, own_cols], rows_v.at[0, 1, pl.ds(0, shard_rows), :], local_sem.at[0]
-    )
-    own_rows.start()
-    gate_swap = send(1, gate_ref, gate_v.at[own_block, :], core_peer)
+    arrivals = []
+    for peer in (y_peer, corner_peer, core_peer):
+        block = pl.ds(pl.multiple_of(peer["dp"] * per_peer, per_peer), per_peer)
+        arrivals.append(send(leaving_place_ref.at[block, :], place_v.at[me], peer))
+        arrivals.append(send(leaving_ref.at[block, :], arrived_v.at[me], peer))
+    block = pl.ds(pl.multiple_of(me * per_peer, per_peer), per_peer)
+    stay_place = pltpu.make_async_copy(
+        leaving_place_ref.at[block, :], place_v.at[me], local_sem.at[4]
+    )
+    stay_place.start()
+    stay = pltpu.make_async_copy(leaving_ref.at[block, :], arrived_v.at[me], local_sem.at[5])
+    stay.start()
+    gate_swap = send(gate_ref, gate_v.at[own_block, :], core_peer)
     gate_own = pltpu.make_async_copy(gate_ref, gate_v.at[own_block, :], local_sem.at[1])
     gate_own.start()
-    up_swap = send(2, up_ref, up_v.at[own_block, :], core_peer)
+    up_swap = send(up_ref, up_v.at[own_block, :], core_peer)
     up_own = pltpu.make_async_copy(up_ref, up_v.at[own_block, :], local_sem.at[2])
     up_own.start()
     down_own = pltpu.make_async_copy(down_ref, down_v, local_sem.at[3])
     down_own.start()
+
+    stay_place.wait()
+    stay.wait()
+    for copy in arrivals:
+        copy.wait_recv()
+    slots = place_v.shape[0] * per_peer
+    places = place_v[...].reshape(slots, place_v.shape[2])
+    land = places.astype(jnp.float32).T.astype(jnp.bfloat16)[:shard_rows]
+    squares = jnp.zeros((shard_rows, 1), jnp.float32)
+    for start in range(0, features, tile):
+        cols = slice(start, start + tile)
+        wide = jnp.dot(
+            land, arrived_v[:, :, cols].reshape(slots, tile), preferred_element_type=jnp.float32
+        )
+        batch_v[:, cols] = wide.astype(jnp.bfloat16)
+        squares = squares + jnp.sum(wide * wide, axis=1, keepdims=True)
+    scale = lax.rsqrt(squares / features + 1e-05)
+    for start in range(0, features, tile):
+        cols = slice(start, start + tile)
+        norm_v[:, cols] = (batch_v[:, cols].astype(jnp.float32) * scale).astype(jnp.bfloat16)
+
+    first = send(norm_v.at[:, peer_cols], rows_v.at[0, 0, pl.ds(0, shard_rows), :], y_peer)
+    own_rows = pltpu.make_async_copy(
+        norm_v.at[:, own_cols], rows_v.at[0, 1, pl.ds(0, shard_rows), :], local_sem.at[0]
+    )
+    own_rows.start()
 
     near = pl.ds(0, shard_rows)
     far = pl.ds(shard_rows, shard_rows)
@@ -162,104 +203,124 @@
 
     def spread(step):
         z_copy[step] = send(
-            2 + step, rows_v.at[0, :, near, :], rows_v.at[step, :, near, :], z_peer[step]
+            rows_v.at[0, :, near, :], rows_v.at[step, :, near, :], z_peer[step]
         )
 
     def cross(step):
         if step:
             z_copy[step].wait_recv()
         x_copy[step] = send(
-            6 + step, rows_v.at[step, :, near, :], rows_v.at[step, :, far, :], x_peer
+            rows_v.at[step, :, near, :], rows_v.at[step, :, far, :], x_peer
         )
 
     parts = {}
 
-    def project(step):
-        x_copy[step].wait_recv()
+    def project(step, compute, pieces):
         for which, weight in ((0, gate_v), (1, up_v)):
-            if step == order[0]:
+            if step == 0 and compute == near:
                 (gate_swap, up_swap)[which].wait_recv()
                 (gate_own, up_own)[which].wait()
 
             def body(i, carry):
                 cols = pl.ds(pl.multiple_of(i * tile, tile), tile)
-                part_out[step, which, :, cols] = jnp.dot(
-                    rows_v[step, 0], weight[:, cols], preferred_element_type=jnp.float32
+                part_out[step, which, compute, cols] = jnp.dot(
+                    rows_v[step, 0, compute, :],
+                    weight[:, cols],
+                    preferred_element_type=jnp.float32,
                 ).astype(jnp.bfloat16)
                 return carry
 
             lax.fori_loop(0, hidden_width // tile, body, 0)
-            parts[step, which] = send(
-                10 + 2 * step + which, part_out.at[step, which], part_in.at[step, which], y_peer
+            if len(pieces) == 1:
+                push(step, which, pieces[0])
+        if len(pieces) > 1:
+            for piece in pieces:
+                push(step, 0, piece)
+                push(step, 1, piece)
+
+    def push(step, which, piece):
+        parts.setdefault((step, piece.start), []).append(
+            send(
+                part_out.at[step, which, piece, :], part_in.at[step, which, piece, :], y_peer
             )
+        )
 
     term_copy, pair_copy = {}, {}
 
-    def finish(step):
-        parts[step, 0].wait_recv()
-        parts[step, 1].wait_recv()
+    def finish(step, rows_cut, pieces):
+        for piece in pieces:
+            for copy in parts[step, piece.start]:
+                copy.wait_recv()
 
         def body(i, carry):
             cols = pl.ds(pl.multiple_of(i * tile, tile), tile)
-            rows = rows_v[step, 1]
+            rows = rows_v[step, 1, rows_cut, :]
             gate_sum = jnp.dot(
                 rows, gate_v[:, cols], preferred_element_type=jnp.float32
-            ) + part_in[step, 0, :, cols].astype(jnp.float32)
+            ) + part_in[step, 0, rows_cut, cols].astype(jnp.float32)
             up_sum = jnp.dot(
                 rows, up_v[:, cols], preferred_element_type=jnp.float32
-            ) + part_in[step, 1, :, cols].astype(jnp.float32)
-            hidden_v[:, cols] = (gate_sum / (1.0 + jnp.exp(-gate_sum)) * up_sum).astype(
+            ) + part_in[step, 1, rows_cut, cols].astype(jnp.float32)
+            hidden_v[rows_cut, cols] = (gate_sum / (1.0 + jnp.exp(-gate_sum)) * up_sum).astype(
                 jnp.bfloat16
             )
             return carry
 
         lax.fori_loop(0, hidden_width // tile, body, 0)
-        if step == order[0]:
+        if step == 0:
             down_own.wait()
 
         def down_body(i, carry):
             cols = pl.ds(pl.multiple_of(i * tile, tile), tile)
-            term_v[step, :, cols] = jnp.dot(
-                hidden_v[...], down_v[:, cols], preferred_element_type=jnp.float32
+            term_v[step, rows_cut, cols] = jnp.dot(
+                hidden_v[rows_cut, :], down_v[:, cols], preferred_element_type=jnp.float32
             ).astype(jnp.bfloat16)
             return carry
 
         lax.fori_loop(0, 2 * half // tile, down_body, 0)
-        term_copy[step] = send(18 + step, term_v.at[step, far, :], x_in.at[step], x_peer)
+        if rows_cut != near:
+            term_copy[step] = send(term_v.at[step, far, :], x_in.at[step], x_peer)
 
     def pair(step):
         term_copy[step].wait_recv()
         term_v[step, near, :] = (
             term_v[step, near, :].astype(jnp.float32) + x_in[step].astype(jnp.float32)
         ).astype(jnp.bfloat16)
-        pair_copy[step] = send(21 + step, term_v.at[step, near, :], z_in.at[step - 1], z_peer[step])
-
-    s0, s1, s2, s3 = order
-    cross(s0)
-    spread(s1)
-    project(s0)
-    spread(s2)
-    cross(s1)
-    project(s1)
-    spread(s3)
-    cross(s2)
-    finish(s0)
-    project(s2)
-    cross(s3)
-    finish(s1)
-    project(s3)
-    pair(s1)
-    finish(s2)
-    pair(s2)
-    finish(s3)
-    pair(s3)
+        pair_copy[step] = send(term_v.at[step, near, :], z_in.at[step - 1], z_peer[step])
+
+    both = pl.ds(0, 2 * shard_rows)
+    cross(0)
+    spread(2)
+    project(0, near, (near,))
+    x_copy[0].wait_recv()
+    project(0, far, (far,))
+    spread(3)
+    cross(2)
+    project(2, near, (near,))
+    x_copy[2].wait_recv()
+    project(2, far, (far,))
+    spread(1)
+    cross(3)
+    finish(0, both, (near, far))
+    x_copy[3].wait_recv()
+    project(3, both, (both,))
+    cross(1)
+    finish(2, both, (near, far))
+    x_copy[1].wait_recv()
+    project(1, both, (far, near))
+    pair(2)
+    finish(3, both, (both,))
+    pair(3)
+    finish(1, far, (far,))
+    finish(1, near, (near,))
+    pair(1)
     term_copy[0].wait_recv()
     total = (
-        batch_ref[...].astype(jnp.float32)
+        batch_v[...].astype(jnp.float32)
         + term_v[0, near, :].astype(jnp.float32)
         + x_in[0].astype(jnp.float32)
     )
-    for step in (s1, s2, s3):
+    for step in (2, 3, 1):
         pair_copy[step].wait_recv()
         total = total + z_in[step - 1].astype(jnp.float32)
     out_ref[...] = total.astype(jnp.bfloat16)
@@ -268,20 +329,34 @@
 
 
 def chip_plan(loader_rows, row_counts, row_targets, gate_weight, up_weight, down_weight):
-    local_batch = rebalance(loader_rows, row_counts, row_targets)
-    travelling = normalize(local_batch)
-    shard_rows, features = local_batch.shape
+    pick_matrix, slot_rows, row_place, is_live, dp_count, per_peer, shard_rows = pick_slots(
+        loader_rows, row_counts, row_targets
+    )
+    features = slot_rows.shape[1]
+    pick = pick_matrix.astype(jnp.bfloat16)
+    lanes = 128
+    place_hot = (row_place[:, None] == jnp.arange(lanes, dtype=jnp.int32)[None, :]).astype(
+        jnp.bfloat16
+    )
+    leaving = jnp.dot(pick, slot_rows, preferred_element_type=jnp.float32).astype(jnp.bfloat16)
+    leaving_place = jnp.dot(pick, place_hot, preferred_element_type=jnp.float32).astype(
+        jnp.bfloat16
+    )
     hidden_width = gate_weight.shape[1]
     half = features // 2
     vmem = pl.BlockSpec(memory_space=pltpu.VMEM)
     any_space = pl.BlockSpec(memory_space=pl.ANY)
     bf16 = jnp.bfloat16
     return pl.pallas_call(
-        functools.partial(ff_kernel, (0, 2, 3, 1)),
+        ff_kernel,
         out_shape=jax.ShapeDtypeStruct((shard_rows, features), bf16),
         in_specs=[vmem, vmem, any_space, any_space, any_space],
         out_specs=vmem,
         scratch_shapes=[
+            pltpu.VMEM((dp_count, per_peer, features), bf16),
+            pltpu.VMEM((dp_count, per_peer, lanes), bf16),
+            pltpu.VMEM((shard_rows, features), bf16),
+            pltpu.VMEM((shard_rows, features), bf16),
             pltpu.VMEM((half, hidden_width), bf16),
             pltpu.VMEM((half, hidden_width), bf16),
             pltpu.VMEM((hidden_width, features), bf16),
@@ -292,17 +367,17 @@
             pltpu.VMEM((4, 2 * shard_rows, features), bf16),
             pltpu.VMEM((4, shard_rows, features), bf16),
             pltpu.VMEM((3, shard_rows, features), bf16),
-            pltpu.SemaphoreType.DMA((4,)),
-            pltpu.SemaphoreType.DMA((25,)),
-            pltpu.SemaphoreType.DMA((25,)),
+            pltpu.SemaphoreType.DMA((6,)),
+            pltpu.SemaphoreType.DMA((40,)),
+            pltpu.SemaphoreType.DMA((40,)),
         ],
         compiler_params=pltpu.CompilerParams(
-            collective_id=0, has_side_effects=True, vmem_limit_bytes=60 * 1024 * 1024
+            collective_id=0, has_side_effects=True, vmem_limit_bytes=62 * 1024 * 1024
         ),
         cost_estimate=pl.CostEstimate(
             flops=26 * 10**9, bytes_accessed=26 * 2**20, transcendentals=2**20
         ),
-    )(travelling, local_batch, gate_weight, up_weight, down_weight)
+    )(leaving, leaving_place, gate_weight, up_weight, down_weight)
 
 
 def per_device(*args):

time: 185 us -> 176 us (0.951)
  Pallas kernels: 152 us -> 169 us
  waiting for transfers between devices: 15.4 us -> 0 us
  starting transfers between devices: 7.75 us -> 0 us
    pallas_call x1, Pallas kernels: 152 us -> 169 us  [chip_plan(): pl.pallas_call(ff_kernel, out_shape=jax.ShapeDtypeStruct((shard_rows, fea...]
    all_to_all x2 -> x0, waiting for transfers between devices: 15.4 us -> none  [the longest x1 13.2 us: rebalance(): lax.all_to_all(outgoing.reshape(dp_count, per_peer, feature_count), 'dp',...]
    all_to_all x2 -> x0, starting transfers between devices: 7.75 us -> none  [the longest x1 4.24 us: rebalance(): lax.all_to_all(out_place.reshape(dp_count, per_peer), 'dp', split_axis=0,...]
  transfers between devices with their start and end apart: 2 -> 0, of which waited for: 2 -> 0; matrix products, arithmetic and copies ran while one was open for 1% -> 0% of each run, Pallas kernels for 0% -> 0%
where the time goes in v3:
time: 176 us; the launch traced here: 175 us
  Pallas kernels  169 us (96%)
  matrix products  2.25 us (1%)
  local copies, waits for them, and re-layouts  1.87 us (1%)
    pallas_call x1, Pallas kernels, chip_plan(): pl.pallas_call(ff_kernel, out_shape=jax.ShapeDtypeStruct((shard_rows, fea...  169 us

profile of v3, /device:TPU:0, one launch (start us, length us, event | category | flops | bytes accessed | tf_op | source)
XLA Modules:
  0.0 175.4 jit_solution(8040053424066324699)
XLA Ops:
  0.0 0.0 copy-start
  0.8 0.7 and_select_fusion
  1.4 0.1 fusion.2
  1.5 0.2 reduce_window_sum.11
  1.7 0.2 select_reduce_fusion
  1.9 0.8 convolution_convert_fusion.1.leaving_place_ref
  2.7 0.0 copy-done
  2.7 1.4 convolution_convert_fusion.leaving_ref
  4.1 169.3 %shard_map.64 = bf16[64,4096]{1,0:T(8,128)(2,1)} custom-call(bf16[128,4096]{1,0:T(8,128)(2,1)} %convolution_convert_fusion.leaving_ref, bf16[128,128]{1,0:T(8,128)(2,1)} %convolution_convert_fusion.1.leaving_place_ref, bf16[1024,2048]{1,0:T(8,128)(2,1)} %gate_ref.1, bf16[1024,2048]{1,0:T(8,128)(2,1)} %up_ref.1, bf16[2048,4096]{1,0:T(8,128)(2,1)} %down_ref.1), custom_call_target="tpu_custom_call" | custom-call | flops 25999998976 | bytes 27262976 | tf_op jit(solution)/shard_map/pallas_call | solution.py:350
  173.5 1.9 %copy.9 = bf16[64,4096]{1,0:T(8,128)(2,1)} copy(bf16[64,4096]{1,0:T(8,128)(2,1)} %shard_map.64) | data formatting | bytes 1048576
  (2 shorter events, 0.0 us)
Async XLA Ops:
  0.0 2.7 %copy-start = (bf16[1,1,128,4096]{3,2,1,0:T(8,128)(2,1)S(1)}, bf16[1,1,128,4096]{3,2,1,0:T(8,128)(2,1)}, u32[]{:S(2)}) copy-start(bf16[1,1,128,4096]{3,2,1,0:T(8,128)(2,1)} %param.6) | copy-start | bytes 3145732

commit v4 on v3

--- a/solution.py
+++ b/solution.py
@@ -101,7 +101,7 @@
 
 def ff_kernel(
     leaving_ref, leaving_place_ref, gate_ref, up_ref, down_ref, out_ref,
-    arrived_v, place_v, batch_v, norm_v, gate_v, up_v, down_v, rows_v, part_out, part_in, hidden_v, term_v, x_in, z_in,
+    arrived_v, place_v, batch_v, norm_v, gate_v, up_v, down_v, rows_v, part_out, own_v, part_in, hidden_v, term_v, x_in, z_in,
     local_sem, send_sem, recv_sem,
 ):
     me = lax.axis_index("dp")
@@ -130,9 +130,10 @@
     pl.semaphore_wait(barrier, 7)
 
     sent = []
+    counter = list(range(send_sem.shape[0]))
 
     def send(src, dst, peer):
-        index = len(sent)
+        index = counter.pop(0)
         copy = pltpu.make_async_remote_copy(
             src_ref=src,
             dst_ref=dst,
@@ -215,19 +216,31 @@
 
     parts = {}
 
-    def project(step, compute, pieces):
+    slot = {0: 0, 2: 1, 3: 0, 1: 1}
+    earlier = {3: 0, 1: 2}
+
+    def project(step, cut, pieces):
+        if step in earlier:
+            for key in parts:
+                if key[0] == earlier[step]:
+                    for copy in parts[key]:
+                        copy.wait_send()
+                        sent[:] = [other for other in sent if other is not copy]
+        count = cut.size
         for which, weight in ((0, gate_v), (1, up_v)):
-            if step == 0 and compute == near:
+            if step == 0 and cut == near:
                 (gate_swap, up_swap)[which].wait_recv()
                 (gate_own, up_own)[which].wait()
 
             def body(i, carry):
                 cols = pl.ds(pl.multiple_of(i * tile, tile), tile)
-                part_out[step, which, compute, cols] = jnp.dot(
-                    rows_v[step, 0, compute, :],
+                act = jnp.dot(
+                    rows_v[step, :, cut, :].reshape(2 * count, half),
                     weight[:, cols],
                     preferred_element_type=jnp.float32,
-                ).astype(jnp.bfloat16)
+                )
+                part_out[slot[step], which, cut, cols] = act[:count].astype(jnp.bfloat16)
+                own_v[slot[step], which, cut, cols] = act[count:]
                 return carry
 
             lax.fori_loop(0, hidden_width // tile, body, 0)
@@ -241,7 +254,7 @@
     def push(step, which, piece):
         parts.setdefault((step, piece.start), []).append(
             send(
-                part_out.at[step, which, piece, :], part_in.at[step, which, piece, :], y_peer
+                part_out.at[slot[step], which, piece, :], part_in.at[step, which, piece, :], y_peer
             )
         )
 
@@ -254,13 +267,12 @@
 
         def body(i, carry):
             cols = pl.ds(pl.multiple_of(i * tile, tile), tile)
-            rows = rows_v[step, 1, rows_cut, :]
-            gate_sum = jnp.dot(
-                rows, gate_v[:, cols], preferred_element_type=jnp.float32
-            ) + part_in[step, 0, rows_cut, cols].astype(jnp.float32)
-            up_sum = jnp.dot(
-                rows, up_v[:, cols], preferred_element_type=jnp.float32
-            ) + part_in[step, 1, rows_cut, cols].astype(jnp.float32)
+            gate_sum = own_v[slot[step], 0, rows_cut, cols] + part_in[
+                step, 0, rows_cut, cols
+            ].astype(jnp.float32)
+            up_sum = own_v[slot[step], 1, rows_cut, cols] + part_in[
+                step, 1, rows_cut, cols
+            ].astype(jnp.float32)
             hidden_v[rows_cut, cols] = (gate_sum / (1.0 + jnp.exp(-gate_sum)) * up_sum).astype(
                 jnp.bfloat16
             )
@@ -296,16 +308,15 @@
     project(0, far, (far,))
     spread(3)
     cross(2)
-    project(2, near, (near,))
     x_copy[2].wait_recv()
-    project(2, far, (far,))
+    project(2, both, (both,))
     spread(1)
     cross(3)
     finish(0, both, (near, far))
     x_copy[3].wait_recv()
     project(3, both, (both,))
     cross(1)
-    finish(2, both, (near, far))
+    finish(2, both, (both,))
     x_copy[1].wait_recv()
     project(1, both, (far, near))
     pair(2)
@@ -361,7 +372,8 @@
             pltpu.VMEM((half, hidden_width), bf16),
             pltpu.VMEM((hidden_width, features), bf16),
             pltpu.VMEM((4, 2, 2 * shard_rows, half), bf16),
-            pltpu.VMEM((4, 2, 2 * shard_rows, hidden_width), bf16),
+            pltpu.VMEM((2, 2, 2 * shard_rows, hidden_width), bf16),
+            pltpu.VMEM((2, 2, 2 * shard_rows, hidden_width), jnp.float32),
             pltpu.VMEM((4, 2, 2 * shard_rows, hidden_width), bf16),
             pltpu.VMEM((2 * shard_rows, hidden_width), bf16),
             pltpu.VMEM((4, 2 * shard_rows, features), bf16),

time: 176 us -> 174 us (0.989)
  no operation moved by 1% of the time
where the time goes in v4:
time: 174 us
  Pallas kernels  168 us (97%)
  matrix products  2.25 us (1%)
  local copies, waits for them, and re-layouts  1.87 us (1%)
    pallas_call x1, Pallas kernels, chip_plan(): pl.pallas_call(ff_kernel, out_shape=jax.ShapeDtypeStruct((shard_rows, fea...  168 us

profile of v4, /device:TPU:0, one launch (start us, length us, event | category | flops | bytes accessed | tf_op | source)
XLA Modules:
  0.0 174.0 jit_solution(12630957830256783094)
XLA Ops:
  0.0 0.0 copy-start
  0.8 0.7 and_select_fusion
  1.4 0.1 fusion.2
  1.5 0.2 reduce_window_sum.11
  1.7 0.2 select_reduce_fusion
  1.9 0.8 convolution_convert_fusion.1.leaving_place_ref
  2.7 0.0 copy-done
  2.7 1.4 convolution_convert_fusion.leaving_ref
  4.1 168.0 %shard_map.64 = bf16[64,4096]{1,0:T(8,128)(2,1)} custom-call(bf16[128,4096]{1,0:T(8,128)(2,1)} %convolution_convert_fusion.leaving_ref, bf16[128,128]{1,0:T(8,128)(2,1)} %convolution_convert_fusion.1.leaving_place_ref, bf16[1024,2048]{1,0:T(8,128)(2,1)} %gate_ref.1, bf16[1024,2048]{1,0:T(8,128)(2,1)} %up_ref.1, bf16[2048,4096]{1,0:T(8,128)(2,1)} %down_ref.1), custom_call_target="tpu_custom_call" | custom-call | flops 25999998976 | bytes 27262976 | tf_op jit(solution)/shard_map/pallas_call | solution.py:361
  172.1 1.9 %copy.9 = bf16[64,4096]{1,0:T(8,128)(2,1)} copy(bf16[64,4096]{1,0:T(8,128)(2,1)} %shard_map.64) | data formatting | bytes 1048576
  (2 shorter events, 0.0 us)
Async XLA Ops:
  0.0 2.7 %copy-start = (bf16[1,1,128,4096]{3,2,1,0:T(8,128)(2,1)S(1)}, bf16[1,1,128,4096]{3,2,1,0:T(8,128)(2,1)}, u32[]{:S(2)}) copy-start(bf16[1,1,128,4096]{3,2,1,0:T(8,128)(2,1)} %param.6) | copy-start | bytes 3145732

commit v5 on v4

--- a/solution.py
+++ b/solution.py
@@ -115,7 +115,6 @@
     z_peer = {
         1: {"tensor": 2 * (z + 1 - 2 * lax.rem(z, 2)) + x},
         2: {"tensor": 2 * lax.rem(z + 2, 4) + x},
-        3: {"tensor": 2 * (3 - z) + x},
     }
     shard_rows, features = batch_v.shape
     half = features // 2
@@ -125,9 +124,9 @@
     tile = 512
 
     barrier = pltpu.get_barrier_semaphore()
-    for peer in (core_peer, y_peer, corner_peer, x_peer, z_peer[1], z_peer[2], z_peer[3]):
+    for peer in (core_peer, y_peer, corner_peer, x_peer, z_peer[1], z_peer[2]):
         pl.semaphore_signal(barrier, inc=1, device_id=peer, device_id_type=MESH)
-    pl.semaphore_wait(barrier, 7)
+    pl.semaphore_wait(barrier, 6)
 
     sent = []
     counter = list(range(send_sem.shape[0]))
@@ -203,12 +202,11 @@
     z_copy, x_copy = {}, {}
 
     def spread(step):
-        z_copy[step] = send(
-            rows_v.at[0, :, near, :], rows_v.at[step, :, near, :], z_peer[step]
-        )
+        source, peer = (2, z_peer[1]) if step == 3 else (0, z_peer[step])
+        z_copy[step] = send(rows_v.at[source, :, near, :], rows_v.at[step, :, near, :], peer)
 
     def cross(step):
-        if step:
+        if step in (1, 3):
             z_copy[step].wait_recv()
         x_copy[step] = send(
             rows_v.at[step, :, near, :], rows_v.at[step, :, far, :], x_peer
@@ -216,8 +214,8 @@
 
     parts = {}
 
-    slot = {0: 0, 2: 1, 3: 0, 1: 1}
-    earlier = {3: 0, 1: 2}
+    slot = {0: 0, 1: 1, 3: 0, 2: 1}
+    earlier = {3: 0, 2: 1}
 
     def project(step, cut, pieces):
         if step in earlier:
@@ -295,43 +293,49 @@
 
     def pair(step):
         term_copy[step].wait_recv()
-        term_v[step, near, :] = (
-            term_v[step, near, :].astype(jnp.float32) + x_in[step].astype(jnp.float32)
-        ).astype(jnp.bfloat16)
-        pair_copy[step] = send(term_v.at[step, near, :], z_in.at[step - 1], z_peer[step])
+        wide = term_v[step, near, :].astype(jnp.float32) + x_in[step].astype(jnp.float32)
+        if step == 2:
+            pair_copy[3].wait_recv()
+            wide = wide + z_in[2].astype(jnp.float32)
+        term_v[step, near, :] = wide.astype(jnp.bfloat16)
+        pair_copy[step] = send(
+            term_v.at[step, near, :], z_in.at[step - 1], z_peer[2 if step == 2 else 1]
+        )
 
     both = pl.ds(0, 2 * shard_rows)
     cross(0)
+    spread(1)
     spread(2)
     project(0, near, (near,))
     x_copy[0].wait_recv()
     project(0, far, (far,))
+    cross(1)
+    project(1, near, (near,))
+    z_copy[2].wait_recv()
     spread(3)
+    x_copy[1].wait_recv()
+    project(1, far, (far,))
+    cross(3)
     cross(2)
-    x_copy[2].wait_recv()
-    project(2, both, (both,))
-    spread(1)
-    cross(3)
     finish(0, both, (near, far))
     x_copy[3].wait_recv()
     project(3, both, (both,))
-    cross(1)
-    finish(2, both, (both,))
-    x_copy[1].wait_recv()
-    project(1, both, (far, near))
-    pair(2)
+    finish(1, both, (near, far))
+    x_copy[2].wait_recv()
+    project(2, both, (far, near))
+    pair(1)
     finish(3, both, (both,))
     pair(3)
-    finish(1, far, (far,))
-    finish(1, near, (near,))
-    pair(1)
+    finish(2, far, (far,))
+    finish(2, near, (near,))
+    pair(2)
     term_copy[0].wait_recv()
     total = (
         batch_v[...].astype(jnp.float32)
         + term_v[0, near, :].astype(jnp.float32)
         + x_in[0].astype(jnp.float32)
     )
-    for step in (2, 3, 1):
+    for step in (1, 2):
         pair_copy[step].wait_recv()
         total = total + z_in[step - 1].astype(jnp.float32)
     out_ref[...] = total.astype(jnp.bfloat16)

time: 174 us -> 176 us (1.011)
  Pallas kernels: 168 us -> 170 us
    pallas_call x1, Pallas kernels: 168 us -> 170 us  [chip_plan(): pl.pallas_call(ff_kernel, out_shape=jax.ShapeDtypeStruct((shard_rows, fea...]
where the time goes in v5:
time: 176 us
  Pallas kernels  170 us (97%)
  matrix products  2.25 us (1%)
  local copies, waits for them, and re-layouts  1.87 us (1%)
    pallas_call x1, Pallas kernels, chip_plan(): pl.pallas_call(ff_kernel, out_shape=jax.ShapeDtypeStruct((shard_rows, fea...  170 us

profile of v5, /device:TPU:0, one launch (start us, length us, event | category | flops | bytes accessed | tf_op | source)
XLA Modules:
  0.0 175.8 jit_solution(8282273524193160889)
XLA Ops:
  0.0 0.0 copy-start
  0.8 0.7 and_select_fusion
  1.4 0.1 fusion.2
  1.5 0.2 reduce_window_sum.11
  1.7 0.2 select_reduce_fusion
  1.9 0.8 convolution_convert_fusion.1.leaving_place_ref
  2.7 0.0 copy-done
  2.7 1.4 convolution_convert_fusion.leaving_ref
  4.1 169.7 %shard_map.64 = bf16[64,4096]{1,0:T(8,128)(2,1)} custom-call(bf16[128,4096]{1,0:T(8,128)(2,1)} %convolution_convert_fusion.leaving_ref, bf16[128,128]{1,0:T(8,128)(2,1)} %convolution_convert_fusion.1.leaving_place_ref, bf16[1024,2048]{1,0:T(8,128)(2,1)} %gate_ref.1, bf16[1024,2048]{1,0:T(8,128)(2,1)} %up_ref.1, bf16[2048,4096]{1,0:T(8,128)(2,1)} %down_ref.1), custom_call_target="tpu_custom_call" | custom-call | flops 25999998976 | bytes 27262976 | tf_op jit(solution)/shard_map/pallas_call | solution.py:365
  173.9 1.9 %copy.9 = bf16[64,4096]{1,0:T(8,128)(2,1)} copy(bf16[64,4096]{1,0:T(8,128)(2,1)} %shard_map.64) | data formatting | bytes 1048576
  (2 shorter events, 0.0 us)
Async XLA Ops:
  0.0 2.7 %copy-start = (bf16[1,1,128,4096]{3,2,1,0:T(8,128)(2,1)S(1)}, bf16[1,1,128,4096]{3,2,1,0:T(8,128)(2,1)}, u32[]{:S(2)}) copy-start(bf16[1,1,128,4096]{3,2,1,0:T(8,128)(2,1)} %param.6) | copy-start | bytes 3145732

commit v6 on v4

--- a/solution.py
+++ b/solution.py
@@ -164,11 +164,6 @@
     gate_swap = send(gate_ref, gate_v.at[own_block, :], core_peer)
     gate_own = pltpu.make_async_copy(gate_ref, gate_v.at[own_block, :], local_sem.at[1])
     gate_own.start()
-    up_swap = send(up_ref, up_v.at[own_block, :], core_peer)
-    up_own = pltpu.make_async_copy(up_ref, up_v.at[own_block, :], local_sem.at[2])
-    up_own.start()
-    down_own = pltpu.make_async_copy(down_ref, down_v, local_sem.at[3])
-    down_own.start()
 
     stay_place.wait()
     stay.wait()
@@ -195,6 +190,11 @@
         norm_v.at[:, own_cols], rows_v.at[0, 1, pl.ds(0, shard_rows), :], local_sem.at[0]
     )
     own_rows.start()
+    up_swap = send(up_ref, up_v.at[own_block, :], core_peer)
+    up_own = pltpu.make_async_copy(up_ref, up_v.at[own_block, :], local_sem.at[2])
+    up_own.start()
+    down_own = pltpu.make_async_copy(down_ref, down_v, local_sem.at[3])
+    down_own.start()
 
     near = pl.ds(0, shard_rows)
     far = pl.ds(shard_rows, shard_rows)

time: 174 us -> 174 us (level)
  no operation moved by 1% of the time
where the time goes in v6:
time: 174 us
  Pallas kernels  168 us (97%)
  matrix products  2.25 us (1%)
  local copies, waits for them, and re-layouts  1.87 us (1%)
    pallas_call x1, Pallas kernels, chip_plan(): pl.pallas_call(ff_kernel, out_shape=jax.ShapeDtypeStruct((shard_rows, fea...  168 us

profile of v6, /device:TPU:0, one launch (start us, length us, event | category | flops | bytes accessed | tf_op | source)
XLA Modules:
  0.0 174.0 jit_solution(16133672107684162730)
XLA Ops:
  0.0 0.0 copy-start
  0.8 0.7 and_select_fusion
  1.4 0.1 fusion.2
  1.5 0.2 reduce_window_sum.11
  1.7 0.2 select_reduce_fusion
  1.9 0.8 convolution_convert_fusion.1.leaving_place_ref
  2.7 0.0 copy-done
  2.7 1.4 convolution_convert_fusion.leaving_ref
  4.1 168.0 %shard_map.64 = bf16[64,4096]{1,0:T(8,128)(2,1)} custom-call(bf16[128,4096]{1,0:T(8,128)(2,1)} %convolution_convert_fusion.leaving_ref, bf16[128,128]{1,0:T(8,128)(2,1)} %convolution_convert_fusion.1.leaving_place_ref, bf16[1024,2048]{1,0:T(8,128)(2,1)} %gate_ref.1, bf16[1024,2048]{1,0:T(8,128)(2,1)} %up_ref.1, bf16[2048,4096]{1,0:T(8,128)(2,1)} %down_ref.1), custom_call_target="tpu_custom_call" | custom-call | flops 25999998976 | bytes 27262976 | tf_op jit(solution)/shard_map/pallas_call | solution.py:361
  172.1 1.9 %copy.9 = bf16[64,4096]{1,0:T(8,128)(2,1)} copy(bf16[64,4096]{1,0:T(8,128)(2,1)} %shard_map.64) | data formatting | bytes 1048576
  (2 shorter events, 0.0 us)
Async XLA Ops:
  0.0 2.7 %copy-start = (bf16[1,1,128,4096]{3,2,1,0:T(8,128)(2,1)S(1)}, bf16[1,1,128,4096]{3,2,1,0:T(8,128)(2,1)}, u32[]{:S(2)}) copy-start(bf16[1,1,128,4096]{3,2,1,0:T(8,128)(2,1)} %param.6) | copy-start | bytes 3145732
